TPU v7x, 128 devices: a whole 4x4x4 slice. The times are simulated.
128 devices in a mesh: section: 2 (over core), row: 4 (over y), col: 16 (over x, z).
Axes of the slice: x: 4, y: 4, z: 4, core: 2. Of those that a mesh axis runs over, the one named last changes fastest.
Arguments:
- activations: bfloat16 [32768, 4096], P(('section', 'col'), 'row'), parts along dimension 0, may hold values from -300 to 300
- out_grads: bfloat16 [2, 32768, 4096], P(None, ('section', 'col')), parts along dimension 1, may hold values from -0.25 to 0.25
- weights: float32 [4, 4096, 4096], P('section', 'col', 'row'), parts along dimension 0, may hold values from -125 to 125
- row_prev: float32 [4, 4096], P('section', 'col'), parts along dimension 0, may hold values from 0.002 to 16
- col_prev: float32 [4, 4096], P('section', 'row'), parts along dimension 0, may hold values from 0.002 to 16
Outputs:
- new_weights: float32 [4, 4096, 4096], P('section', 'col', 'row'), parts along dimension 0
- direction: bfloat16 [4, 4096, 4096], P('section', 'col', 'row'), parts along dimension 0
- row_factor: float32 [4, 4096], P('section', 'col'), parts along dimension 0
- col_factor: float32 [4, 4096], P('section', 'row'), parts along dimension 0
- update_rms: float32 [4], P('section'), parts along dimension 0
- param_rms: float32 [4], P('section'), parts along dimension 0
There are 2 independent parts, one for each index of `section`. A program takes and returns all parts, laid end to end along the dimension named above; each array names one. Nothing has to cross between parts.
All inputs are finite; a program needn't handle non-finite values.
Results may differ from a plain program's by a relative error of at most 0.019.
Values may be sent and summed in bfloat16 or wider, within the bound.
No kernel may reach another device: no remote copies, remote signals or barrier semaphores. Data moves between devices by JAX's collectives and lax.ppermute only.
A program may use at most 128 MiB of HBM per device.

v0:
```python
import jax
import jax.numpy as jnp
from jax import lax
from jax.sharding import PartitionSpec as P

D = 4096
INNER = 4096


decay_rate = 1.0 - 100.0 ** (-0.8)
square_eps = 1e-30
step_scale = 0.01
clip_limit = 1.0


def one_term(cotangent, activations):
    return lax.dot_general(
        cotangent, activations, (((0,), (0,)), ((), ())), preferred_element_type=jnp.float32
    )


def body(activations, out_grads, weights, row_prev, col_prev):
    matrices = weights.shape[0]
    entry_count = INNER * D
    gradients = []
    for number in range(matrices):
        gradients.append(
            lax.psum_scatter(
                one_term(out_grads[number], activations).astype(jnp.bfloat16),
                "col",
                scatter_dimension=0,
                tiled=True,
            ).astype(jnp.float32)
        )
    param_squares = jnp.sum(weights * weights, axis=(1, 2))
    param_totals = lax.psum(param_squares, ("row", "col"))
    scaled_list = []
    row_list = []
    col_list = []
    for number in range(matrices):
        gradient = gradients[number]
        square = gradient * gradient + square_eps
        row_sum = lax.psum(jnp.sum(square, axis=1), "row")
        col_sum = lax.psum(jnp.sum(square, axis=0), "col")
        row_new = decay_rate * row_prev[number] + (1.0 - decay_rate) * row_sum / D
        col_new = decay_rate * col_prev[number] + (1.0 - decay_rate) * col_sum / INNER
        row_mean = lax.psum(jnp.sum(row_new), "col") / INNER
        scaled_list.append(gradient / jnp.sqrt(row_new[:, None] * col_new[None, :] / row_mean))
        row_list.append(row_new)
        col_list.append(col_new)
    totals_list = [lax.psum(jnp.sum(scaled * scaled), ("row", "col")) for scaled in scaled_list]
    updated = []
    directions = []
    update_list = []
    param_list = []
    for number in range(matrices):
        update_scale = jnp.sqrt(totals_list[number] / entry_count + 1e-06)
        clipped = scaled_list[number] / jnp.maximum(1.0, update_scale / clip_limit)
        param_scale = jnp.sqrt(param_totals[number] / entry_count + 1e-06)
        updated.append(weights[number] - step_scale * param_scale * clipped)
        directions.append(clipped.astype(jnp.bfloat16))
        update_list.append(update_scale)
        param_list.append(param_scale)
    return (
        jnp.stack(updated),
        jnp.stack(directions),
        jnp.stack(row_list),
        jnp.stack(col_list),
        jnp.stack(update_list),
        jnp.stack(param_list),
    )


def solution(mesh):
    placed = (
        P(("section", "col"), "row"),
        P(None, ("section", "col"), None),
        P("section", "col", "row"),
        P("section", "col"),
        P("section", "row"),
    )
    return jax.shard_map(
        body,
        mesh=mesh,
        in_specs=placed,
        out_specs=(
            P("section", "col", "row"),
            P("section", "col", "row"),
            P("section", "col"),
            P("section", "row"),
            P("section"),
            P("section"),
        ),
        check_vma=False,
    )
```

profile of v0, /device:TPU:32, one launch (start us, length us, event | category | flops | bytes accessed | tf_op | source)
XLA Modules:
  0.0 446.8 jit_solution(11997632572667159022)
XLA Ops:
  7.2 0.0 copy-start
  7.2 0.0 reduce-scatter.3.cloned.1.call-start
  7.2 1.5 copy-done
  8.8 14.6 %fusion.6 = bf16[4096,1024]{1,0:T(8,128)(2,1)} fusion(bf16[1024,1024]{1,0:T(8,128)(2,1)S(1)} %copy-done, bf16[2,1024,4096]{2,1,0:T(8,128)(2,1)} %param.6), kind=kOutput, calls=%fused_computation.6 | convolution fusion | flops 8594128896 | bytes 18874368 | tf_op jit(solution)/shard_map/dot_general | solution.py:17
  23.4 0.0 reduce-scatter.3.cloned.1.call-update
  23.4 0.0 reduce-scatter.5.cloned.1.call-start
  23.5 14.6 %fusion.9 = bf16[4096,1024]{1,0:T(8,128)(2,1)} fusion(bf16[1024,1024]{1,0:T(8,128)(2,1)S(1)} %copy-done, bf16[2,1024,4096]{2,1,0:T(8,128)(2,1)} %param.6), kind=kOutput, calls=%fused_computation.7 | convolution fusion | flops 8594128896 | bytes 18874368 | tf_op jit(solution)/shard_map/dot_general | solution.py:17
  38.0 0.0 copy-start.2
  38.0 0.0 copy-start.1
  38.0 0.0 reduce-scatter.5.cloned.1.call-update
  38.1 2.0 multiply_reduce_fusion
  40.0 0.0 copy-done.2
  40.0 0.0 copy-done.1
  40.1 70.6 %reduce-scatter.3.cloned.1.call-done = bf16[256,1024]{1,0:T(8,128)(2,1)} async-done(((bf16[4096,1024]{1,0:T(8,128)(2,1)}), bf16[256,1024]{1,0:T(8,128)(2,1)}) %reduce-scatter.3.cloned.1.call-update) | async-done | bytes 524304 | tf_op jit(solution)/shard_map/reduce_scatter | solution.py:28
  110.7 1.3 fusion.13
  112.0 86.5 %reduce-scatter.5.cloned.1.call-done = bf16[256,1024]{1,0:T(8,128)(2,1)} async-done(((bf16[4096,1024]{1,0:T(8,128)(2,1)}), bf16[256,1024]{1,0:T(8,128)(2,1)}) %reduce-scatter.5.cloned.1.call-update) | async-done | bytes 524304 | tf_op jit(solution)/shard_map/reduce_scatter | solution.py:28
  198.6 1.3 fusion.16
  199.9 10.5 %all-reduce.2 = (f32[256]{0:T(256)S(1)}, f32[256]{0:T(256)S(1)}) all-reduce(f32[256]{0:T(256)S(1)} %get-tuple-element.9, f32[256]{0:T(256)S(1)} %get-tuple-element.7), channel_id=1, replica_groups=mesh['section'=2,'row'=4,'col'=16] {'row'}, use_global_device_ids=true, to_apply=%region_13.0 | all-reduce | flops 512 | bytes 4096 | tf_op jit(solution)/shard_map/psum | solution.py:43
  210.4 0.6 fusion.20
  211.0 37.7 %all-reduce.1 = (f32[]{:T(128)}, f32[1024]{0:T(1024)S(1)}, f32[]{:T(128)}, f32[1024]{0:T(1024)S(1)}) all-reduce(f32[]{:T(128)} %get-tuple-element.33, f32[1024]{0:T(1024)S(1)} %get-tuple-element.8, f32[]{:T(128)} %get-tuple-element.19, f32[1024]{0:T(1024)S(1)} %get-tuple-element.6), channel_id=1, replica_groups=mesh['section'=2,'row'=4,'col'=16] {'col'}, use_global_device_ids=true, to_apply=%region_17.0 | all-reduce | flops 2050 | bytes 16400 | tf_op jit(solution)/shard_map/psum | solution.py:47
  250.0 2.1 multiply_reduce_fusion.2
  252.1 2.1 multiply_reduce_fusion.1
  254.2 175.0 %all-reduce = (f32[2]{0:T(128)S(1)}, f32[]{:T(128)}, f32[]{:T(128)}) all-reduce(f32[2]{0:T(128)S(1)} %multiply_reduce_fusion, f32[]{:T(128)} %multiply_reduce_fusion.1, f32[]{:T(128)} %multiply_reduce_fusion.2), channel_id=1, replica_groups=mesh['section'=2,'row'=4,'col'=16] {'row','col'}, use_global_device_ids=true, to_apply=%region_1.0 | all-reduce | flops 4 | bytes 32 | tf_op jit(solution)/shard_map/psum | solution.py:36
  429.2 0.6 fusion.22
  431.2 0.6 pad_maximum_fusion.5
  433.2 0.6 pad_maximum_fusion.4
  433.8 0.6 pad_maximum_fusion.2
  434.4 2.5 fusion.19
  436.9 1.1 pad_maximum_fusion.1
  437.9 1.5 pad_maximum_fusion
  439.4 0.6 pad_maximum_fusion.3
  (4 shorter events, 0.0 us)
Async XLA Ops:
  7.2 1.6 copy-start
  7.2 103.5 %reduce-scatter.3.cloned.1.call-start = ((), (), s32[]{:S(2)}) async-start(), calls=%async_computation.2 | async-start | bytes 8912896 | tf_op jit(solution)/shard_map/reduce_scatter | solution.py:28
  23.4 175.1 %reduce-scatter.5.cloned.1.call-start = ((), (), s32[]{:S(2)}) async-start(), calls=%async_computation.3 | async-start | bytes 8912896 | tf_op jit(solution)/shard_map/reduce_scatter | solution.py:28
  38.0 2.0 copy-start.2
  38.0 2.0 copy-start.1
Sparse Core Ops, SparseCore 0:
  23.5 87.1 reduce-scatter.2
  114.1 84.4 reduce-scatter.4
where the time goes:
time: 447 us
  blocking collectives  223 us (50%)
  waiting for transfers between devices  157 us (35%)
  matrix products  29.2 us (7%)
  between operations  18.2 us (4%)
  other arithmetic  16.8 us (4%)
    psum x1, blocking collectives, body(): param_totals = lax.psum(param_squares, ('row', 'col'))  175 us
    reduce_scatter x2, waiting for transfers between devices, body(): lax.psum_scatter(one_term(out_grads[number], activations).astype(jnp.bflo...  157 us
    psum x1, blocking collectives, body(): row_mean = lax.psum(jnp.sum(row_new), 'col') / INNER  37.7 us
    dot_general x2, matrix products, one_term(): lax.dot_general(cotangent, activations, (((0,), (0,)), ((), ())), preferr...  29.2 us
    psum x1, blocking collectives, body(): row_sum = lax.psum(jnp.sum(square, axis=1), 'row')  10.5 us
  transfers between devices with their start and end apart: 2, of which 2 were waited for; matrix products, arithmetic and copies ran while one was open for 4% of the time, Pallas kernels for 0%

commit v1 on v0

v1 whole, which is shorter than its diff:
```python
import functools

import jax
import jax.numpy as jnp
from jax import lax
from jax.experimental import pallas as pl
from jax.experimental.pallas import tpu as pltpu
from jax.sharding import PartitionSpec as P

D = 4096
INNER = 4096
SIDE = 4
TILE = 256

decay_rate = 1.0 - 100.0 ** (-0.8)
square_eps = 1e-30
step_scale = 0.01
clip_limit = 1.0
f32 = jnp.float32
bf16 = jnp.bfloat16


def multiply(blocks, x_ref, targets):
    for part, block in enumerate(blocks):
        term = lax.dot_general(
            block[0], x_ref[...], (((0,), (0,)), ((), ())), preferred_element_type=f32
        ).astype(bf16)
        targets[0][part, 0] = term[:, :TILE]
        targets[1][part, 0] = term[:, TILE:]


def product_kernel(count, here, d0, d1, d2, d3, x_ref, *targets):
    if count == 1:
        multiply((d0, d1, d2, d3), x_ref, targets)
        return
    for chunk in range(count):

        @pl.when(pl.program_id(0) == chunk)
        def _():
            multiply((d0, d1, d2, d3), x_ref, targets[2 * chunk : 2 * chunk + 2])


def products(here, out_grads, activations, axis, offsets):
    count = len(offsets)
    mats, tokens, _ = out_grads.shape

    def block_spec(part):
        def index(c, m, t):
            along = t[0] >> 2 if axis == 0 else t[0]
            across = t[0] if axis == 0 else t[0] >> 2
            offset = offsets[0]
            for k in range(1, count):
                offset = jnp.where(c == k, offsets[k], offset)
            along = (along + offset) & 3
            across = (across + OTHER[part]) & 3
            block = along * SIDE + across if axis == 0 else across * SIDE + along
            return (m, 0, block)

        return pl.BlockSpec((1, tokens, TILE), index)

    def out_spec(k):
        def index(c, m, t):
            place = jnp.where(c == k, m, jnp.where(c < k, 0, mats - 1)) if count > 1 else m
            return (0, place, 0, 0)

        return pl.BlockSpec((SIDE, 1, TILE, TILE), index)

    out_type = jax.ShapeDtypeStruct((SIDE, mats, TILE, TILE), bf16)
    return pl.pallas_call(
        functools.partial(product_kernel, count),
        grid_spec=pltpu.PrefetchScalarGridSpec(
            num_scalar_prefetch=1,
            grid=(count, mats),
            in_specs=[block_spec(part) for part in range(SIDE)]
            + [pl.BlockSpec((tokens, 2 * TILE), lambda c, m, t: (0, axis))],
            out_specs=[out_spec(k) for k in range(count) for _ in (0, 1)],
        ),
        out_shape=[out_type] * (2 * count),
        compiler_params=pltpu.CompilerParams(vmem_limit_bytes=40 * 2**20),
        cost_estimate=pl.CostEstimate(
            flops=count * mats * 2 * 1024 * 1024 * 512,
            bytes_accessed=count * mats * 3 * 2**20,
            transcendentals=0,
        ),
    )(here, out_grads, out_grads, out_grads, out_grads, activations)


def shift_pairs(axis, step):
    pairs = []
    for x in range(SIDE):
        for z in range(SIDE):
            to = ((x + step) % SIDE, z) if axis == 0 else (x, (z + step) % SIDE)
            pairs.append((x * SIDE + z, to[0] * SIDE + to[1]))
    return pairs


def send(value, axis, step):
    return lax.ppermute(value, "col", shift_pairs(axis, step))


def after(value, *others):
    return lax.optimization_barrier((value,) + others)[0]


def add(*values):
    total = values[0].astype(f32)
    for value in values[1:]:
        total = total + value.astype(f32)
    return total


OTHER = (2, 1, 3, 0)
PARTS = (slice(0, 3), slice(3, 4))


def body(activations, out_grads, weights, row_prev, col_prev):
    mats = weights.shape[0]
    here = lax.axis_index("col").astype(jnp.int32).reshape(1)
    both = (0, 1)

    got1 = []
    for axis in both:
        low, high = products(here, out_grads, activations, axis, (2,))
        got1.append((send(low, axis, 1), send(high, axis, -1)))
    near = [products(here, out_grads, activations, axis, (1, 3)) for axis in both]
    got2, got3 = [], []
    for axis in both:
        low_next, high_next, low_last, high_last = near[axis]
        up, down = got1[axis]
        high_next, low_last, up, down = lax.optimization_barrier((high_next, low_last, up, down))
        got2.append((send(high_next, axis, 1), send(low_last, axis, -1)))
        plus = [add(low_next[s], up[s]).astype(bf16) for s in PARTS]
        minus = [add(high_last[s], down[s]).astype(bf16) for s in PARTS]
        first = (send(plus[0], axis, 1), send(minus[0], axis, -1))
        last = lax.optimization_barrier((plus[1], minus[1]) + first)
        got3.append((last[2:], (send(last[0], axis, 1), send(last[1], axis, -1))))
    own = []
    for axis in both:
        own.append(products(after(here, got1[1][0]), out_grads, activations, axis, (0,)))
    reduced = []
    for axis in both:
        for k in both:
            reduced.append(
                [
                    add(own[axis][k][s], got3[axis][n][k], got2[axis][1 - k][s])
                    for n, s in enumerate(PARTS)
                ]
            )
    got4 = []
    for axis in both:
        low = reduced[2 * axis][0].astype(bf16)
        high = reduced[2 * axis + 1][0].astype(bf16)
        plus = jnp.stack([low[0], high[1]])
        minus = jnp.stack([high[0], low[2]])
        got4.append((send(plus, 1 - axis, 1), send(minus, 1 - axis, -1)))
    pieces = []
    for axis in both:
        low, high = reduced[2 * axis], reduced[2 * axis + 1]
        up, down = got4[axis]
        plus = add(low[0][1].astype(bf16), up[0]).astype(bf16)
        minus = add(high[0][2].astype(bf16), down[0]).astype(bf16)
        up5, down5 = send(plus, 1 - axis, 1), send(minus, 1 - axis, -1)
        pieces.append(low[1][0] + add(up5, down[1]))
        pieces.append(high[1][0] + add(down5, up[1]))
    gradient = jnp.concatenate(pieces, axis=2)

    param_squares = jnp.sum(weights * weights, axis=(1, 2))
    pure = gradient * gradient
    square = pure + square_eps
    stage = jnp.concatenate([jnp.sum(square, axis=2).reshape(-1), param_squares])
    stage = lax.psum(stage, "row")
    row_sum = stage[: mats * TILE].reshape(mats, TILE)
    param_part = stage[mats * TILE :]
    row_new = decay_rate * row_prev + (1.0 - decay_rate) * row_sum / D
    col_part = jnp.sum(square, axis=1)
    mix_part = jnp.sum(pure * (1.0 / row_new)[:, :, None], axis=1)
    scalars = jnp.concatenate([jnp.sum(row_new, axis=1), param_part])
    payload = jnp.concatenate(
        [
            col_part.reshape(-1, 128),
            mix_part.reshape(-1, 128),
            jnp.pad(scalars, (0, 8 * 128 - 2 * mats)).reshape(8, 128),
        ]
    )
    gathered = lax.all_to_all(
        jnp.broadcast_to(payload[None], (SIDE * SIDE,) + payload.shape), "col", 0, 0
    )
    total = jnp.sum(gathered, axis=0)
    lines = mats * 1024 // 128
    col_sum = total[:lines].reshape(mats, 1024)
    mix_sum = total[lines : 2 * lines].reshape(mats, 1024)
    row_mean = total[2 * lines, :mats] / INNER
    param_totals = total[2 * lines, mats : 2 * mats]
    col_new = decay_rate * col_prev + (1.0 - decay_rate) * col_sum / INNER
    scaled_total = lax.psum(jnp.sum(mix_sum / col_new, axis=1), "row") * row_mean
    entry_count = INNER * D
    update_scale = jnp.sqrt(scaled_total / entry_count + 1e-06)
    param_scale = jnp.sqrt(param_totals / entry_count + 1e-06)
    shrink = jnp.sqrt(row_mean) / jnp.maximum(1.0, update_scale / clip_limit)
    row_factor = lax.rsqrt(row_new)
    col_factor = lax.rsqrt(col_new) * shrink[:, None]
    clipped = gradient * row_factor[:, :, None] * col_factor[:, None, :]
    updated = weights - (step_scale * param_scale)[:, None, None] * clipped
    return updated, clipped.astype(bf16), row_new, col_new, update_scale, param_scale


def solution(mesh):
    placed = (
        P(("section", "col"), "row"),
        P(None, ("section", "col"), None),
        P("section", "col", "row"),
        P("section", "col"),
        P("section", "row"),
    )
    return jax.shard_map(
        body,
        mesh=mesh,
        in_specs=placed,
        out_specs=(
            P("section", "col", "row"),
            P("section", "col", "row"),
            P("section", "col"),
            P("section", "row"),
            P("section"),
            P("section"),
        ),
        check_vma=False,
    )
```

time: 447 us -> 167 us (0.37)
  blocking collectives: 223 us -> 32.2 us
  waiting for transfers between devices: 157 us -> 50.4 us
  starting transfers between devices: 0.08 us -> 35.7 us
  Pallas kernels: 0 us -> 32.5 us
  matrix products: 29.2 us -> 0 us
  between operations: 18.2 us -> 1.01 us
  other arithmetic: 16.8 us -> 11.2 us
    psum x3 -> x2, blocking collectives: 223 us -> 18.4 us  [the longest x1 10.7 us: body(): stage = lax.psum(stage, 'row')]
    reduce_scatter x2 -> x0, waiting for transfers between devices: 157 us -> none  [body(): lax.psum_scatter(one_term(out_grads[number], activations).astype(jnp.bflo...]
    ppermute x0 -> x24, waiting for transfers between devices: none -> 50.4 us  [send(): return lax.ppermute(value, 'col', shift_pairs(axis, step))]
    ppermute x0 -> x24, starting transfers between devices: none -> 35.7 us  [send(): return lax.ppermute(value, 'col', shift_pairs(axis, step))]
    pallas_call x0 -> x6, Pallas kernels: none -> 32.5 us  [products(): pl.pallas_call(functools.partial(product_kernel, count), grid_spec=pltpu....]
    dot_general x2 -> x0, matrix products: 29.2 us -> none  [one_term(): lax.dot_general(cotangent, activations, (((0,), (0,)), ((), ())), preferr...]
    all_to_all x0 -> x1, blocking collectives: none -> 13.8 us  [body(): lax.all_to_all(jnp.broadcast_to(payload[None], (SIDE * SIDE,) + payload.s...]
    convert_element_type x0 -> x13, other arithmetic: none -> 7.52 us  [the longest x1 3.68 us: body(): clipped.astype(bf16)]
  transfers between devices with their start and end apart: 2 -> 24, of which waited for: 2 -> 12; matrix products, arithmetic and copies ran while one was open for 4% -> 3% of each run, Pallas kernels for 0% -> 17%
where the time goes in v1:
time: 167 us; the launch traced here: 165 us
  waiting for transfers between devices  50.4 us (30%)
  starting transfers between devices  35.7 us (21%)
  Pallas kernels  32.5 us (19%)
  blocking collectives  32.2 us (19%)
  other arithmetic  11.2 us (7%)
  local copies, waits for them, and re-layouts  1.85 us (1%)
    ppermute x24, waiting for transfers between devices, send(): return lax.ppermute(value, 'col', shift_pairs(axis, step))  50.4 us
    ppermute x24, starting transfers between devices, send(): return lax.ppermute(value, 'col', shift_pairs(axis, step))  35.7 us
    pallas_call x6, Pallas kernels, products(): pl.pallas_call(functools.partial(product_kernel, count), grid_spec=pltpu....  32.5 us
    all_to_all x1, blocking collectives, body(): lax.all_to_all(jnp.broadcast_to(payload[None], (SIDE * SIDE,) + payload.s...  13.8 us
    psum x1, blocking collectives, body(): stage = lax.psum(stage, 'row')  10.7 us
    psum x1, blocking collectives, body(): lax.psum(jnp.sum(mix_sum / col_new, axis=1), 'row') * row_mean  7.75 us
    convert_element_type x1, other arithmetic, body(): clipped.astype(bf16)  3.68 us
  transfers between devices with their start and end apart: 24, of which 12 were waited for; matrix products, arithmetic and copies ran while one was open for 3% of the time, Pallas kernels for 17%

profile of v1, /device:TPU:32, one launch (start us, length us, event | category | flops | bytes accessed | tf_op | source)
XLA Modules:
  0.0 165.0 jit_solution(150229267787595197)
XLA Ops:
  0.6 1.6 copy-done
  2.2 4.4 %shard_map.100 = (bf16[4,2,256,256]{3,2,1,0:T(8,128)(2,1)S(1)}, bf16[4,2,256,256]{3,2,1,0:T(8,128)(2,1)S(1)}) custom-call(s32[1]{0:T(128)} %bitcast.here, bf16[2,1024,4096]{2,1,0:T(8,128)(2,1)} %d3.11, bf16[2,1024,4096]{2,1,0:T(8,128)(2,1)} %d3.11, bf16[2,1024,4096]{2,1,0:T(8,128)(2,1)} %d3.11, bf16[2,1024,4096]{2,1,0:T(8,128)(2,1)} %d3.11, ...), custom_call_target="tpu_custom_call" | custom-call | flops 2147483648 | bytes 6291456 | tf_op jit(solution)/shard_map/pallas_call | solution.py:69
  6.6 2.0 %collective-permute-start = (bf16[4,2,256,256]{3,2,1,0:T(8,128)(2,1)S(1)}, bf16[4,2,256,256]{3,2,1,0:T(8,128)(2,1)S(1)}, u32[]{:S(2)}, u32[]{:S(2)}) collective-permute-start(bf16[4,2,256,256]{3,2,1,0:T(8,128)(2,1)S(1)} %get-tuple-element.39), channel_id=1, source_target_pairs={{0,1},{1,2},{2,3},{3,0},{4,5},{5,6},{6,7},{7,4},{8,9},{9,10},{10,1... | collective-permute-start | bytes 3145736 | tf_op jit(solution)/shard_map/ppermute | solution.py:98
  8.7 4.3 %shard_map.103 = (bf16[4,2,256,256]{3,2,1,0:T(8,128)(2,1)S(1)}, bf16[4,2,256,256]{3,2,1,0:T(8,128)(2,1)S(1)}) custom-call(s32[1]{0:T(128)} %bitcast.here, bf16[2,1024,4096]{2,1,0:T(8,128)(2,1)} %d3.11, bf16[2,1024,4096]{2,1,0:T(8,128)(2,1)} %d3.11, bf16[2,1024,4096]{2,1,0:T(8,128)(2,1)} %d3.11, bf16[2,1024,4096]{2,1,0:T(8,128)(2,1)} %d3.11, ...), custom_call_target="tpu_custom_call" | custom-call | flops 2147483648 | bytes 6291456 | tf_op jit(solution)/shard_map/pallas_call | solution.py:69
  13.0 1.6 collective-permute-start.1
  14.6 1.7 %collective-permute-start.2 = (bf16[4,2,256,256]{3,2,1,0:T(8,128)(2,1)S(1)}, bf16[4,2,256,256]{3,2,1,0:T(8,128)(2,1)S(1)}, u32[]{:S(2)}, u32[]{:S(2)}) collective-permute-start(bf16[4,2,256,256]{3,2,1,0:T(8,128)(2,1)S(1)} %get-tuple-element.46), channel_id=1, source_target_pairs={{0,12},{1,13},{2,14},{3,15},{4,0},{5,1},{6,2},{7,3},{8,4},{9,5},{1... | collective-permute-start | bytes 3145736 | tf_op jit(solution)/shard_map/ppermute | solution.py:98
  16.3 7.5 %shard_map.105 = (bf16[4,2,256,256]{3,2,1,0:T(8,128)(2,1)S(1)}, bf16[4,2,256,256]{3,2,1,0:T(8,128)(2,1)S(1)}, bf16[4,2,256,256]{3,2,1,0:T(8,128)(2,1)S(1)}, bf16[4,2,256,256]{3,2,1,0:T(8,128)(2,1)S(1)}) custom-call(s32[1]{0:T(128)} %bitcast.here, bf16[2,1024,4096]{2,1,0:T(8,128)(2,1)} %d3.11, bf16[2,1024,4096]{2,1,0:T(8,128)(2,1)} %d3.11, ...), custom_call_target="tpu_custom_call" | custom-call | flops 4294967296 | bytes 12582912 | tf_op jit(solution)/shard_map/pallas_call | solution.py:69
  23.9 0.4 multiply_reduce_fusion.1
  24.3 7.6 %shard_map.102 = (bf16[4,2,256,256]{3,2,1,0:T(8,128)(2,1)S(1)}, bf16[4,2,256,256]{3,2,1,0:T(8,128)(2,1)S(1)}, bf16[4,2,256,256]{3,2,1,0:T(8,128)(2,1)S(1)}, bf16[4,2,256,256]{3,2,1,0:T(8,128)(2,1)S(1)}) custom-call(s32[1]{0:T(128)} %bitcast.here, bf16[2,1024,4096]{2,1,0:T(8,128)(2,1)} %d3.11, bf16[2,1024,4096]{2,1,0:T(8,128)(2,1)} %d3.11, ...), custom_call_target="tpu_custom_call" | custom-call | flops 4294967296 | bytes 12582912 | tf_op jit(solution)/shard_map/pallas_call | solution.py:69
  31.8 1.4 collective-permute-done.13
  33.2 0.2 add_convert_fusion.3
  33.4 1.7 %collective-permute-start.14 = (bf16[3,2,256,256]{3,2,1,0:T(8,128)(2,1)S(1)}, bf16[3,2,256,256]{3,2,1,0:T(8,128)(2,1)S(1)}, u32[]{:S(2)}, u32[]{:S(2)}) collective-permute-start(bf16[3,2,256,256]{3,2,1,0:T(8,128)(2,1)S(1)} %add_convert_fusion.3), channel_id=1, source_target_pairs={{0,1},{1,2},{2,3},{3,0},{4,5},{5,6},{6,7},{7,4},{8,9},{9,10},{10,1... | collective-permute-start | bytes 2359304 | tf_op jit(solution)/shard_map/ppermute | solution.py:98
  35.1 0.2 add_convert_fusion.2
  35.3 0.5 collective-permute-start.15
  35.8 2.1 %collective-permute-start.17 = (bf16[4,2,256,256]{3,2,1,0:T(8,128)(2,1)S(1)}, bf16[4,2,256,256]{3,2,1,0:T(8,128)(2,1)S(1)}, u32[]{:S(2)}, u32[]{:S(2)}) collective-permute-start(bf16[4,2,256,256]{3,2,1,0:T(8,128)(2,1)S(1)} %get-tuple-element.66), channel_id=1, source_target_pairs={{0,3},{1,0},{2,1},{3,2},{4,7},{5,4},{6,5},{7,6},{8,11},{9,8},{10,9... | collective-permute-start | bytes 3145736 | tf_op jit(solution)/shard_map/ppermute | solution.py:98
  37.9 0.9 collective-permute-done.1
  38.8 1.7 %collective-permute-start.18 = (bf16[4,2,256,256]{3,2,1,0:T(8,128)(2,1)S(1)}, bf16[4,2,256,256]{3,2,1,0:T(8,128)(2,1)S(1)}, u32[]{:S(2)}, u32[]{:S(2)}) collective-permute-start(bf16[4,2,256,256]{3,2,1,0:T(8,128)(2,1)S(1)} %get-tuple-element.70), channel_id=1, source_target_pairs={{0,1},{1,2},{2,3},{3,0},{4,5},{5,6},{6,7},{7,4},{8,9},{9,10},{10,1... | collective-permute-start | bytes 3145736 | tf_op jit(solution)/shard_map/ppermute | solution.py:98
  40.6 1.1 add_convert_fusion.7
  41.7 0.3 collective-permute-start.3
  42.0 1.1 add_convert_fusion.6
  43.1 10.9 %collective-permute-done.14 = bf16[3,2,256,256]{3,2,1,0:T(8,128)(2,1)S(1)} collective-permute-done((bf16[3,2,256,256]{3,2,1,0:T(8,128)(2,1)S(1)}, bf16[3,2,256,256]{3,2,1,0:T(8,128)(2,1)S(1)}, u32[]{:S(2)}, u32[]{:S(2)}) %collective-permute-start.14) | collective-permute-done | bytes 786464 | tf_op jit(solution)/shard_map/ppermute | solution.py:98
  54.0 2.8 %collective-permute-start.4 = (bf16[3,2,256,256]{3,2,1,0:T(8,128)(2,1)}, bf16[3,2,256,256]{3,2,1,0:T(8,128)(2,1)S(1)}, u32[]{:S(2)}, u32[]{:S(2)}) collective-permute-start(bf16[3,2,256,256]{3,2,1,0:T(8,128)(2,1)} %add_convert_fusion.6), channel_id=1, source_target_pairs={{0,12},{1,13},{2,14},{3,15},{4,0},{5,1},{6,2},{7,3},{8,4},{9,5},{1... | collective-permute-start | bytes 2359304 | tf_op jit(solution)/shard_map/ppermute | solution.py:98
  56.7 4.4 %shard_map.104 = (bf16[4,2,256,256]{3,2,1,0:T(8,128)(2,1)S(1)}, bf16[4,2,256,256]{3,2,1,0:T(8,128)(2,1)S(1)}) custom-call(s32[1]{0:T(128)} %bitcast.here, bf16[2,1024,4096]{2,1,0:T(8,128)(2,1)} %d3.11, bf16[2,1024,4096]{2,1,0:T(8,128)(2,1)} %d3.11, bf16[2,1024,4096]{2,1,0:T(8,128)(2,1)} %d3.11, bf16[2,1024,4096]{2,1,0:T(8,128)(2,1)} %d3.11, ...), custom_call_target="tpu_custom_call" | custom-call | flops 2147483648 | bytes 6291456 | tf_op jit(solution)/shard_map/pallas_call | solution.py:69
  61.1 4.4 %shard_map.101 = (bf16[4,2,256,256]{3,2,1,0:T(8,128)(2,1)S(1)}, bf16[4,2,256,256]{3,2,1,0:T(8,128)(2,1)S(1)}) custom-call(s32[1]{0:T(128)} %bitcast.here, bf16[2,1024,4096]{2,1,0:T(8,128)(2,1)} %d3.11, bf16[2,1024,4096]{2,1,0:T(8,128)(2,1)} %d3.11, bf16[2,1024,4096]{2,1,0:T(8,128)(2,1)} %d3.11, bf16[2,1024,4096]{2,1,0:T(8,128)(2,1)} %d3.11, ...), custom_call_target="tpu_custom_call" | custom-call | flops 2147483648 | bytes 6291456 | tf_op jit(solution)/shard_map/pallas_call | solution.py:69
  65.5 0.1 add_convert_fusion.10
  65.6 0.1 add_convert_fusion.14
  65.8 0.9 collective-permute-start.6
  66.7 1.2 collective-permute-start.7
  67.9 7.2 %collective-permute-done.4 = bf16[3,2,256,256]{3,2,1,0:T(8,128)(2,1)S(1)} collective-permute-done((bf16[3,2,256,256]{3,2,1,0:T(8,128)(2,1)}, bf16[3,2,256,256]{3,2,1,0:T(8,128)(2,1)S(1)}, u32[]{:S(2)}, u32[]{:S(2)}) %collective-permute-start.4) | collective-permute-done | bytes 786464 | tf_op jit(solution)/shard_map/ppermute | solution.py:98
  75.0 2.0 %collective-permute-start.22 = (bf16[1,2,256,256]{3,2,1,0:T(8,128)(2,1)S(1)}, bf16[1,2,256,256]{3,2,1,0:T(8,128)(2,1)S(1)}, u32[]{:S(2)}, u32[]{:S(2)}) collective-permute-start(bf16[1,2,256,256]{3,2,1,0:T(8,128)(2,1)S(1)} %get-tuple-element.71), channel_id=1, source_target_pairs={{0,3},{1,0},{2,1},{3,2},{4,7},{5,4},{6,5},{7,6},{8,11},{9,8},{10,9... | collective-permute-start | bytes 786440 | tf_op jit(solution)/shard_map/ppermute | solution.py:98
  77.0 1.3 collective-permute-done.17
  78.4 1.6 collective-permute-start.16
  79.9 0.3 add_convert_fusion.1
  80.3 0.3 add_convert_fusion
  80.7 2.8 %collective-permute-start.21 = (bf16[2,2,256,256]{3,2,1,0:T(8,128)(2,1)S(1)}, bf16[2,2,256,256]{3,2,1,0:T(8,128)(2,1)S(1)}, u32[]{:S(2)}, u32[]{:S(2)}) collective-permute-start(bf16[2,2,256,256]{3,2,1,0:T(8,128)(2,1)S(1)} %pad_maximum_fusion.4), channel_id=1, source_target_pairs={{0,12},{1,13},{2,14},{3,15},{4,0},{5,1},{6,2},{7,3},{8,4},{9,5},{1... | collective-permute-start | bytes 1572872 | tf_op jit(solution)/shard_map/ppermute | solution.py:98
  83.6 13.7 %collective-permute-done.6 = bf16[4,2,256,256]{3,2,1,0:T(8,128)(2,1)S(1)} collective-permute-done((bf16[4,2,256,256]{3,2,1,0:T(8,128)(2,1)S(1)}, bf16[4,2,256,256]{3,2,1,0:T(8,128)(2,1)S(1)}, u32[]{:S(2)}, u32[]{:S(2)}) %collective-permute-start.6) | collective-permute-done | bytes 1048608 | tf_op jit(solution)/shard_map/ppermute | solution.py:98
  97.3 1.2 collective-permute-start.19
  98.5 0.3 add_convert_fusion.5
  98.9 0.3 add_convert_fusion.4
  99.4 2.1 %collective-permute-start.10 = (bf16[2,2,256,256]{3,2,1,0:T(8,128)(2,1)S(1)}, bf16[2,2,256,256]{3,2,1,0:T(8,128)(2,1)S(1)}, u32[]{:S(2)}, u32[]{:S(2)}) collective-permute-start(bf16[2,2,256,256]{3,2,1,0:T(8,128)(2,1)S(1)} %pad_maximum_fusion.2), channel_id=1, source_target_pairs={{0,3},{1,0},{2,1},{3,2},{4,7},{5,4},{6,5},{7,6},{8,11},{9,8},{10,9... | collective-permute-start | bytes 1572872 | tf_op jit(solution)/shard_map/ppermute | solution.py:98
  101.5 2.3 %collective-permute-done.21 = bf16[2,2,256,256]{3,2,1,0:T(8,128)(2,1)S(1)} collective-permute-done((bf16[2,2,256,256]{3,2,1,0:T(8,128)(2,1)S(1)}, bf16[2,2,256,256]{3,2,1,0:T(8,128)(2,1)S(1)}, u32[]{:S(2)}, u32[]{:S(2)}) %collective-permute-start.21) | collective-permute-done | bytes 524320 | tf_op jit(solution)/shard_map/ppermute | solution.py:98
  103.8 0.7 collective-permute-start.8
  104.6 3.5 %collective-permute-done.19 = bf16[2,2,256,256]{3,2,1,0:T(8,128)(2,1)S(1)} collective-permute-done((bf16[2,2,256,256]{3,2,1,0:T(8,128)(2,1)S(1)}, bf16[2,2,256,256]{3,2,1,0:T(8,128)(2,1)S(1)}, u32[]{:S(2)}, u32[]{:S(2)}) %collective-permute-start.19) | collective-permute-done | bytes 524320 | tf_op jit(solution)/shard_map/ppermute | solution.py:98
  108.2 2.0 %collective-permute-start.11 = (bf16[1,2,256,256]{3,2,1,0:T(8,128)(2,1)S(1)}, bf16[1,2,256,256]{3,2,1,0:T(8,128)(2,1)S(1)}, u32[]{:S(2)}, u32[]{:S(2)}) collective-permute-start(bf16[1,2,256,256]{3,2,1,0:T(8,128)(2,1)S(1)} %get-tuple-element.56), channel_id=1, source_target_pairs={{0,12},{1,13},{2,14},{3,15},{4,0},{5,1},{6,2},{7,3},{8,4},{9,5},{1... | collective-permute-start | bytes 786440 | tf_op jit(solution)/shard_map/ppermute | solution.py:98
  110.3 0.8 collective-permute-start.23
  111.2 3.0 %collective-permute-done.8 = bf16[2,2,256,256]{3,2,1,0:T(8,128)(2,1)S(1)} collective-permute-done((bf16[2,2,256,256]{3,2,1,0:T(8,128)(2,1)S(1)}, bf16[2,2,256,256]{3,2,1,0:T(8,128)(2,1)S(1)}, u32[]{:S(2)}, u32[]{:S(2)}) %collective-permute-start.8) | collective-permute-done | bytes 524320 | tf_op jit(solution)/shard_map/ppermute | solution.py:98
  114.1 1.9 %collective-permute-start.5 = (bf16[1,2,256,256]{3,2,1,0:T(8,128)(2,1)S(1)}, bf16[1,2,256,256]{3,2,1,0:T(8,128)(2,1)S(1)}, u32[]{:S(2)}, u32[]{:S(2)}) collective-permute-start(bf16[1,2,256,256]{3,2,1,0:T(8,128)(2,1)S(1)} %get-tuple-element.50), channel_id=1, source_target_pairs={{0,4},{1,5},{2,6},{3,7},{4,8},{5,9},{6,10},{7,11},{8,12},{9,13},{1... | collective-permute-start | bytes 786440 | tf_op jit(solution)/shard_map/ppermute | solution.py:98
  116.2 0.9 collective-permute-start.20
  117.1 0.3 collective-permute-done.23
  117.4 3.0 %collective-permute-start.12 = (bf16[2,256,256]{2,1,0:T(8,128)(2,1)S(1)}, bf16[2,256,256]{2,1,0:T(8,128)(2,1)S(1)}, u32[]{:S(2)}, u32[]{:S(2)}) collective-permute-start(bf16[2,256,256]{2,1,0:T(8,128)(2,1)S(1)} %fusion.6), channel_id=1, source_target_pairs={{0,3},{1,0},{2,1},{3,2},{4,7},{5,4},{6,5},{7,6},{8,11},{9,8},{10,9... | collective-permute-start | bytes 786440 | tf_op jit(solution)/shard_map/ppermute | solution.py:98
  120.3 0.2 fusion.1
  120.6 4.2 %collective-permute-done.20 = bf16[2,256,256]{2,1,0:T(8,128)(2,1)S(1)} collective-permute-done((bf16[2,256,256]{2,1,0:T(8,128)(2,1)S(1)}, bf16[2,256,256]{2,1,0:T(8,128)(2,1)S(1)}, u32[]{:S(2)}, u32[]{:S(2)}) %collective-permute-start.20) | collective-permute-done | bytes 262176 | tf_op jit(solution)/shard_map/ppermute | solution.py:98
  124.8 0.2 fusion.2
  125.0 0.2 fusion.3
  125.2 1.8 %collective-permute-done.9 = bf16[2,256,256]{2,1,0:T(8,128)(2,1)S(1)} collective-permute-done((bf16[2,256,256]{2,1,0:T(8,128)(2,1)S(1)}, bf16[2,256,256]{2,1,0:T(8,128)(2,1)S(1)}, u32[]{:S(2)}, u32[]{:S(2)}) %collective-permute-start.9) | collective-permute-done | bytes 262176 | tf_op jit(solution)/shard_map/ppermute | solution.py:98
  127.0 0.2 fusion.4
  127.1 0.5 add_reduce_fusion.1
  127.6 10.7 %psum.14 = f32[514]{0:T(1024)S(1)} all-reduce(f32[514]{0:T(1024)S(1)} %pad_maximum_fusion.6), channel_id=1, replica_groups=mesh['section'=2,'row'=4,'col'=16] {'row'}, use_global_device_ids=true, to_apply=%region_3.0 | all-reduce | flops 514 | bytes 4112 | tf_op jit(solution)/shard_map/psum | solution.py:171
  138.5 0.3 multiply_reduce_fusion
  138.9 13.8 %all_to_all.5 = f32[16,40,128]{2,1,0:T(8,128)S(1)} all-to-all(f32[16,40,128]{2,1,0:T(8,128)S(1)} %broadcast_in_dim.2), channel_id=1, replica_groups=mesh['section'=2,'row'=4,'col'=16] {'col'}, dimensions={0} | all-to-all | bytes 655360 | tf_op jit(solution)/shard_map/all_to_all | solution.py:185
  152.8 0.1 divide_reduce_fusion
  152.9 7.7 %psum.15 = f32[2]{0:T(128)S(1)} all-reduce(f32[2]{0:T(128)S(1)} %get-tuple-element.80), channel_id=1, replica_groups=mesh['section'=2,'row'=4,'col'=16] {'row'}, use_global_device_ids=true, to_apply=%region_8.9 | all-reduce | flops 2 | bytes 16 | tf_op jit(solution)/shard_map/psum | solution.py:195
  160.7 0.6 broadcast_multiply_fusion
  161.3 3.7 %fusion = (bf16[2,256,1024]{2,1,0:T(8,128)(2,1)}, f32[2,256,1024]{2,1,0:T(8,128)}) fusion(f32[2,1024]{1,0:T(2,128)S(1)} %rsqrt_multiply_fusion, f32[2,256]{1,0:T(2,128)S(1)} %get-tuple-element.76, f32[2,256,256]{2,1,0:T(8,128)S(1)} %fusion.1, f32[2,256,256]{2,1,0:T(8,128)S(1)} %fusion.2, f32[2,256,256]{2,1,0:T(8,128)S(1)} %fusion.3, ...), kind=kLoop, calls=%fused_computation.7 | loop fusion | flops 4194304 | bytes 7350280 | tf_op jit(solution)/shard_map/convert_element_type | solution.py:204
  (54 shorter events, 1.3 us)
Async XLA Ops:
  0.6 1.6 copy-start
  6.6 25.2 %collective-permute-start = (bf16[4,2,256,256]{3,2,1,0:T(8,128)(2,1)S(1)}, bf16[4,2,256,256]{3,2,1,0:T(8,128)(2,1)S(1)}, u32[]{:S(2)}, u32[]{:S(2)}) collective-permute-start(bf16[4,2,256,256]{3,2,1,0:T(8,128)(2,1)S(1)} %get-tuple-element.39), channel_id=1, source_target_pairs={{0,1},{1,2},{2,3},{3,0},{4,5},{5,6},{6,7},{7,4},{8,9},{9,10},{10,1... | collective-permute-start | bytes 3145736 | tf_op jit(solution)/shard_map/ppermute | solution.py:98
  8.6 24.6 %collective-permute-start.13 = (bf16[4,2,256,256]{3,2,1,0:T(8,128)(2,1)S(1)}, bf16[4,2,256,256]{3,2,1,0:T(8,128)(2,1)S(1)}, u32[]{:S(2)}, u32[]{:S(2)}) collective-permute-start(bf16[4,2,256,256]{3,2,1,0:T(8,128)(2,1)S(1)} %get-tuple-element.61), channel_id=1, source_target_pairs={{0,3},{1,0},{2,1},{3,2},{4,7},{5,4},{6,5},{7,6},{8,11},{9,8},{10,9... | collective-permute-start | bytes 3145736 | tf_op jit(solution)/shard_map/ppermute | solution.py:98
  13.0 25.8 %collective-permute-start.1 = (bf16[4,2,256,256]{3,2,1,0:T(8,128)(2,1)S(1)}, bf16[4,2,256,256]{3,2,1,0:T(8,128)(2,1)S(1)}, u32[]{:S(2)}, u32[]{:S(2)}) collective-permute-start(bf16[4,2,256,256]{3,2,1,0:T(8,128)(2,1)S(1)} %get-tuple-element.45), channel_id=1, source_target_pairs={{0,4},{1,5},{2,6},{3,7},{4,8},{5,9},{6,10},{7,11},{8,12},{9,13},{1... | collective-permute-start | bytes 3145736 | tf_op jit(solution)/shard_map/ppermute | solution.py:98
  14.6 9.3 %copy-start.1 = (f32[2,256,1024]{2,1,0:T(8,128)S(1)}, f32[2,256,1024]{2,1,0:T(8,128)}, u32[]{:S(2)}) copy-start(f32[2,256,1024]{2,1,0:T(8,128)} %param.7) | copy-start | bytes 6291460
  14.6 26.0 %collective-permute-start.2 = (bf16[4,2,256,256]{3,2,1,0:T(8,128)(2,1)S(1)}, bf16[4,2,256,256]{3,2,1,0:T(8,128)(2,1)S(1)}, u32[]{:S(2)}, u32[]{:S(2)}) collective-permute-start(bf16[4,2,256,256]{3,2,1,0:T(8,128)(2,1)S(1)} %get-tuple-element.46), channel_id=1, source_target_pairs={{0,12},{1,13},{2,14},{3,15},{4,0},{5,1},{6,2},{7,3},{8,4},{9,5},{1... | collective-permute-start | bytes 3145736 | tf_op jit(solution)/shard_map/ppermute | solution.py:98
  33.4 20.5 %collective-permute-start.14 = (bf16[3,2,256,256]{3,2,1,0:T(8,128)(2,1)S(1)}, bf16[3,2,256,256]{3,2,1,0:T(8,128)(2,1)S(1)}, u32[]{:S(2)}, u32[]{:S(2)}) collective-permute-start(bf16[3,2,256,256]{3,2,1,0:T(8,128)(2,1)S(1)} %add_convert_fusion.3), channel_id=1, source_target_pairs={{0,1},{1,2},{2,3},{3,0},{4,5},{5,6},{6,7},{7,4},{8,9},{9,10},{10,1... | collective-permute-start | bytes 2359304 | tf_op jit(solution)/shard_map/ppermute | solution.py:98
  35.3 30.4 %collective-permute-start.15 = (bf16[3,2,256,256]{3,2,1,0:T(8,128)(2,1)S(1)}, bf16[3,2,256,256]{3,2,1,0:T(8,128)(2,1)S(1)}, u32[]{:S(2)}, u32[]{:S(2)}) collective-permute-start(bf16[3,2,256,256]{3,2,1,0:T(8,128)(2,1)S(1)} %add_convert_fusion.2), channel_id=1, source_target_pairs={{0,3},{1,0},{2,1},{3,2},{4,7},{5,4},{6,5},{7,6},{8,11},{9,8},{10,9... | collective-permute-start | bytes 2359304 | tf_op jit(solution)/shard_map/ppermute | solution.py:98
  35.8 42.5 %collective-permute-start.17 = (bf16[4,2,256,256]{3,2,1,0:T(8,128)(2,1)S(1)}, bf16[4,2,256,256]{3,2,1,0:T(8,128)(2,1)S(1)}, u32[]{:S(2)}, u32[]{:S(2)}) collective-permute-start(bf16[4,2,256,256]{3,2,1,0:T(8,128)(2,1)S(1)} %get-tuple-element.66), channel_id=1, source_target_pairs={{0,3},{1,0},{2,1},{3,2},{4,7},{5,4},{6,5},{7,6},{8,11},{9,8},{10,9... | collective-permute-start | bytes 3145736 | tf_op jit(solution)/shard_map/ppermute | solution.py:98
  38.8 41.4 %collective-permute-start.18 = (bf16[4,2,256,256]{3,2,1,0:T(8,128)(2,1)S(1)}, bf16[4,2,256,256]{3,2,1,0:T(8,128)(2,1)S(1)}, u32[]{:S(2)}, u32[]{:S(2)}) collective-permute-start(bf16[4,2,256,256]{3,2,1,0:T(8,128)(2,1)S(1)} %get-tuple-element.70), channel_id=1, source_target_pairs={{0,1},{1,2},{2,3},{3,0},{4,5},{5,6},{6,7},{7,4},{8,9},{9,10},{10,1... | collective-permute-start | bytes 3145736 | tf_op jit(solution)/shard_map/ppermute | solution.py:98
  41.7 25.0 %collective-permute-start.3 = (bf16[3,2,256,256]{3,2,1,0:T(8,128)(2,1)}, bf16[3,2,256,256]{3,2,1,0:T(8,128)(2,1)S(1)}, u32[]{:S(2)}, u32[]{:S(2)}) collective-permute-start(bf16[3,2,256,256]{3,2,1,0:T(8,128)(2,1)} %add_convert_fusion.7), channel_id=1, source_target_pairs={{0,4},{1,5},{2,6},{3,7},{4,8},{5,9},{6,10},{7,11},{8,12},{9,13},{1... | collective-permute-start | bytes 2359304 | tf_op jit(solution)/shard_map/ppermute | solution.py:98
  54.0 21.1 %collective-permute-start.4 = (bf16[3,2,256,256]{3,2,1,0:T(8,128)(2,1)}, bf16[3,2,256,256]{3,2,1,0:T(8,128)(2,1)S(1)}, u32[]{:S(2)}, u32[]{:S(2)}) collective-permute-start(bf16[3,2,256,256]{3,2,1,0:T(8,128)(2,1)} %add_convert_fusion.6), channel_id=1, source_target_pairs={{0,12},{1,13},{2,14},{3,15},{4,0},{5,1},{6,2},{7,3},{8,4},{9,5},{1... | collective-permute-start | bytes 2359304 | tf_op jit(solution)/shard_map/ppermute | solution.py:98
  65.8 31.5 %collective-permute-start.6 = (bf16[4,2,256,256]{3,2,1,0:T(8,128)(2,1)S(1)}, bf16[4,2,256,256]{3,2,1,0:T(8,128)(2,1)S(1)}, u32[]{:S(2)}, u32[]{:S(2)}) collective-permute-start(bf16[4,2,256,256]{3,2,1,0:T(8,128)(2,1)S(1)} %get-tuple-element.51), channel_id=1, source_target_pairs={{0,12},{1,13},{2,14},{3,15},{4,0},{5,1},{6,2},{7,3},{8,4},{9,5},{1... | collective-permute-start | bytes 3145736 | tf_op jit(solution)/shard_map/ppermute | solution.py:98
  66.7 32.2 %collective-permute-start.7 = (bf16[4,2,256,256]{3,2,1,0:T(8,128)(2,1)S(1)}, bf16[4,2,256,256]{3,2,1,0:T(8,128)(2,1)S(1)}, u32[]{:S(2)}, u32[]{:S(2)}) collective-permute-start(bf16[4,2,256,256]{3,2,1,0:T(8,128)(2,1)S(1)} %get-tuple-element.55), channel_id=1, source_target_pairs={{0,4},{1,5},{2,6},{3,7},{4,8},{5,9},{6,10},{7,11},{8,12},{9,13},{1... | collective-permute-start | bytes 3145736 | tf_op jit(solution)/shard_map/ppermute | solution.py:98
  75.0 41.1 %collective-permute-start.22 = (bf16[1,2,256,256]{3,2,1,0:T(8,128)(2,1)S(1)}, bf16[1,2,256,256]{3,2,1,0:T(8,128)(2,1)S(1)}, u32[]{:S(2)}, u32[]{:S(2)}) collective-permute-start(bf16[1,2,256,256]{3,2,1,0:T(8,128)(2,1)S(1)} %get-tuple-element.71), channel_id=1, source_target_pairs={{0,3},{1,0},{2,1},{3,2},{4,7},{5,4},{6,5},{7,6},{8,11},{9,8},{10,9... | collective-permute-start | bytes 786440 | tf_op jit(solution)/shard_map/ppermute | solution.py:98
  78.4 42.1 %collective-permute-start.16 = (bf16[1,2,256,256]{3,2,1,0:T(8,128)(2,1)S(1)}, bf16[1,2,256,256]{3,2,1,0:T(8,128)(2,1)S(1)}, u32[]{:S(2)}, u32[]{:S(2)}) collective-permute-start(bf16[1,2,256,256]{3,2,1,0:T(8,128)(2,1)S(1)} %get-tuple-element.65), channel_id=1, source_target_pairs={{0,1},{1,2},{2,3},{3,0},{4,5},{5,6},{6,7},{7,4},{8,9},{9,10},{10,1... | collective-permute-start | bytes 786440 | tf_op jit(solution)/shard_map/ppermute | solution.py:98
  80.7 23.1 %collective-permute-start.21 = (bf16[2,2,256,256]{3,2,1,0:T(8,128)(2,1)S(1)}, bf16[2,2,256,256]{3,2,1,0:T(8,128)(2,1)S(1)}, u32[]{:S(2)}, u32[]{:S(2)}) collective-permute-start(bf16[2,2,256,256]{3,2,1,0:T(8,128)(2,1)S(1)} %pad_maximum_fusion.4), channel_id=1, source_target_pairs={{0,12},{1,13},{2,14},{3,15},{4,0},{5,1},{6,2},{7,3},{8,4},{9,5},{1... | collective-permute-start | bytes 1572872 | tf_op jit(solution)/shard_map/ppermute | solution.py:98
  97.3 10.8 %collective-permute-start.19 = (bf16[2,2,256,256]{3,2,1,0:T(8,128)(2,1)S(1)}, bf16[2,2,256,256]{3,2,1,0:T(8,128)(2,1)S(1)}, u32[]{:S(2)}, u32[]{:S(2)}) collective-permute-start(bf16[2,2,256,256]{3,2,1,0:T(8,128)(2,1)S(1)} %pad_maximum_fusion.3), channel_id=1, source_target_pairs={{0,4},{1,5},{2,6},{3,7},{4,8},{5,9},{6,10},{7,11},{8,12},{9,13},{1... | collective-permute-start | bytes 1572872 | tf_op jit(solution)/shard_map/ppermute | solution.py:98
  99.4 10.9 %collective-permute-start.10 = (bf16[2,2,256,256]{3,2,1,0:T(8,128)(2,1)S(1)}, bf16[2,2,256,256]{3,2,1,0:T(8,128)(2,1)S(1)}, u32[]{:S(2)}, u32[]{:S(2)}) collective-permute-start(bf16[2,2,256,256]{3,2,1,0:T(8,128)(2,1)S(1)} %pad_maximum_fusion.2), channel_id=1, source_target_pairs={{0,3},{1,0},{2,1},{3,2},{4,7},{5,4},{6,5},{7,6},{8,11},{9,8},{10,9... | collective-permute-start | bytes 1572872 | tf_op jit(solution)/shard_map/ppermute | solution.py:98
  103.8 10.3 %collective-permute-start.8 = (bf16[2,2,256,256]{3,2,1,0:T(8,128)(2,1)S(1)}, bf16[2,2,256,256]{3,2,1,0:T(8,128)(2,1)S(1)}, u32[]{:S(2)}, u32[]{:S(2)}) collective-permute-start(bf16[2,2,256,256]{3,2,1,0:T(8,128)(2,1)S(1)} %pad_maximum_fusion.1), channel_id=1, source_target_pairs={{0,1},{1,2},{2,3},{3,0},{4,5},{5,6},{6,7},{7,4},{8,9},{9,10},{10,1... | collective-permute-start | bytes 1572872 | tf_op jit(solution)/shard_map/ppermute | solution.py:98
  108.2 16.8 %collective-permute-start.11 = (bf16[1,2,256,256]{3,2,1,0:T(8,128)(2,1)S(1)}, bf16[1,2,256,256]{3,2,1,0:T(8,128)(2,1)S(1)}, u32[]{:S(2)}, u32[]{:S(2)}) collective-permute-start(bf16[1,2,256,256]{3,2,1,0:T(8,128)(2,1)S(1)} %get-tuple-element.56), channel_id=1, source_target_pairs={{0,12},{1,13},{2,14},{3,15},{4,0},{5,1},{6,2},{7,3},{8,4},{9,5},{1... | collective-permute-start | bytes 786440 | tf_op jit(solution)/shard_map/ppermute | solution.py:98
  110.3 7.1 %collective-permute-start.23 = (bf16[2,256,256]{2,1,0:T(8,128)(2,1)S(1)}, bf16[2,256,256]{2,1,0:T(8,128)(2,1)S(1)}, u32[]{:S(2)}, u32[]{:S(2)}) collective-permute-start(bf16[2,256,256]{2,1,0:T(8,128)(2,1)S(1)} %fusion.8), channel_id=1, source_target_pairs={{0,12},{1,13},{2,14},{3,15},{4,0},{5,1},{6,2},{7,3},{8,4},{9,5},{1... | collective-permute-start | bytes 786440 | tf_op jit(solution)/shard_map/ppermute | solution.py:98
  114.1 11.1 %collective-permute-start.5 = (bf16[1,2,256,256]{3,2,1,0:T(8,128)(2,1)S(1)}, bf16[1,2,256,256]{3,2,1,0:T(8,128)(2,1)S(1)}, u32[]{:S(2)}, u32[]{:S(2)}) collective-permute-start(bf16[1,2,256,256]{3,2,1,0:T(8,128)(2,1)S(1)} %get-tuple-element.50), channel_id=1, source_target_pairs={{0,4},{1,5},{2,6},{3,7},{4,8},{5,9},{6,10},{7,11},{8,12},{9,13},{1... | collective-permute-start | bytes 786440 | tf_op jit(solution)/shard_map/ppermute | solution.py:98
  116.2 8.6 %collective-permute-start.20 = (bf16[2,256,256]{2,1,0:T(8,128)(2,1)S(1)}, bf16[2,256,256]{2,1,0:T(8,128)(2,1)S(1)}, u32[]{:S(2)}, u32[]{:S(2)}) collective-permute-start(bf16[2,256,256]{2,1,0:T(8,128)(2,1)S(1)} %fusion.7), channel_id=1, source_target_pairs={{0,4},{1,5},{2,6},{3,7},{4,8},{5,9},{6,10},{7,11},{8,12},{9,13},{1... | collective-permute-start | bytes 786440 | tf_op jit(solution)/shard_map/ppermute | solution.py:98
  117.4 7.6 %collective-permute-start.12 = (bf16[2,256,256]{2,1,0:T(8,128)(2,1)S(1)}, bf16[2,256,256]{2,1,0:T(8,128)(2,1)S(1)}, u32[]{:S(2)}, u32[]{:S(2)}) collective-permute-start(bf16[2,256,256]{2,1,0:T(8,128)(2,1)S(1)} %fusion.6), channel_id=1, source_target_pairs={{0,3},{1,0},{2,1},{3,2},{4,7},{5,4},{6,5},{7,6},{8,11},{9,8},{10,9... | collective-permute-start | bytes 786440 | tf_op jit(solution)/shard_map/ppermute | solution.py:98
  120.5 6.4 %collective-permute-start.9 = (bf16[2,256,256]{2,1,0:T(8,128)(2,1)S(1)}, bf16[2,256,256]{2,1,0:T(8,128)(2,1)S(1)}, u32[]{:S(2)}, u32[]{:S(2)}) collective-permute-start(bf16[2,256,256]{2,1,0:T(8,128)(2,1)S(1)} %fusion.5), channel_id=1, source_target_pairs={{0,1},{1,2},{2,3},{3,0},{4,5},{5,6},{6,7},{7,4},{8,9},{9,10},{10,1... | collective-permute-start | bytes 786440 | tf_op jit(solution)/shard_map/ppermute | solution.py:98
  125.2 13.2 %copy-start.5 = (f32[2,256]{1,0:T(2,128)S(1)}, f32[2,256]{1,0:T(2,128)}, u32[]{:S(2)}) copy-start(f32[2,256]{1,0:T(2,128)} %param.8) | copy-start | bytes 6148
  127.6 25.2 %copy-start.4 = (f32[2,1024]{1,0:T(2,128)S(1)}, f32[2,1024]{1,0:T(2,128)}, u32[]{:S(2)}) copy-start(f32[2,1024]{1,0:T(2,128)} %param.9) | copy-start | bytes 24580
  138.4 26.6 %copy-start.3 = (f32[2,256]{1,0:T(2,128)}, f32[2,256]{1,0:T(2,128)S(1)}, u32[]{:S(2)}) copy-start(f32[2,256]{1,0:T(2,128)S(1)} %get-tuple-element.77) | copy-start | bytes 6148
  152.9 12.1 %copy-start.2 = (f32[2,1024]{1,0:T(2,128)}, f32[2,1024]{1,0:T(2,128)S(1)}, u32[]{:S(2)}) copy-start(f32[2,1024]{1,0:T(2,128)S(1)} %get-tuple-element.81) | copy-start | bytes 24580

commit v2 on v1

v2 whole, which is shorter than its diff:
```python
import functools

import jax
import jax.numpy as jnp
from jax import lax
from jax.experimental import pallas as pl
from jax.experimental.pallas import tpu as pltpu
from jax.sharding import PartitionSpec as P

D = 4096
INNER = 4096
SIDE = 4
TILE = 256

decay_rate = 1.0 - 100.0 ** (-0.8)
square_eps = 1e-30
step_scale = 0.01
clip_limit = 1.0
f32 = jnp.float32
bf16 = jnp.bfloat16


def chunk_kernel(near, here, d0, d1, d2, d3, x_ref, *targets):
    blocks = jnp.concatenate([d0[0], d1[0], d2[0], d3[0]], axis=1)
    term = lax.dot_general(
        blocks, x_ref[...], (((0,), (0,)), ((), ())), preferred_element_type=f32
    ).astype(bf16)

    def store(target, *columns):
        for part in range(SIDE):
            rows = slice(part * TILE, (part + 1) * TILE)
            if len(columns) == 1:
                target[part, 0] = term[rows, columns[0]]
            else:
                target[0, part, 0] = term[rows, columns[0]]
                target[1, part, 0] = term[rows, columns[1]]

    lower, upper = slice(0, TILE), slice(TILE, 2 * TILE)
    if near:
        pl.when(pl.program_id(1) == 0)(lambda: store(targets[0], upper, lower))
        pl.when(pl.program_id(1) == 1)(lambda: store(targets[1], lower, upper))
    else:
        store(targets[0], lower)
        store(targets[1], upper)


def feature_block(here, axis, offset, part):
    along = here >> 2 if axis == 0 else here
    across = here if axis == 0 else here >> 2
    along = (along + offset) & 3
    across = (across + OTHER[part]) & 3
    return along * SIDE + across if axis == 0 else across * SIDE + along


def chunk_products(here, out_grads, activations, axis, offsets):
    near = len(offsets) == 2
    mats, tokens, _ = out_grads.shape

    def block_spec(part):
        def index(m, c, t):
            offset = jnp.where(c == 0, offsets[0], offsets[1]) if near else offsets[0]
            return (m, 0, feature_block(t[0], axis, offset, part))

        return pl.BlockSpec((1, tokens, TILE), index)

    shape, block = (SIDE, mats, TILE, TILE), (SIDE, 1, TILE, TILE)
    out_spec = pl.BlockSpec(block, lambda m, c, t: (0, m, 0, 0))
    if near:
        shape, block = (2,) + shape, (2,) + block
        out_spec = pl.BlockSpec(block, lambda m, c, t: (0, 0, m, 0, 0))
    return pl.pallas_call(
        functools.partial(chunk_kernel, near),
        grid_spec=pltpu.PrefetchScalarGridSpec(
            num_scalar_prefetch=1,
            grid=(mats, len(offsets)),
            in_specs=[block_spec(part) for part in range(SIDE)]
            + [pl.BlockSpec((tokens, 2 * TILE), lambda m, c, t: (0, axis))],
            out_specs=[out_spec] * 2,
        ),
        out_shape=[jax.ShapeDtypeStruct(shape, bf16)] * 2,
        compiler_params=pltpu.CompilerParams(vmem_limit_bytes=40 * 2**20),
    )(here, out_grads, out_grads, out_grads, out_grads, activations)


def shift_pairs(axis, step):
    pairs = []
    for x in range(SIDE):
        for z in range(SIDE):
            to = ((x + step) % SIDE, z) if axis == 0 else (x, (z + step) % SIDE)
            pairs.append((x * SIDE + z, to[0] * SIDE + to[1]))
    return pairs


def send(value, axis, step):
    return lax.ppermute(value, "col", shift_pairs(axis, step))


def after(value, *others):
    return lax.optimization_barrier((value,) + others)[0]


def together(values):
    return lax.optimization_barrier(values)


def add(*values):
    total = values[0].astype(f32)
    for value in values[1:]:
        total = total + value.astype(f32)
    return total


OTHER = (2, 1, 3, 0)
ORDER = (1, 0)


def body(activations, out_grads, weights, row_prev, col_prev):
    mats = weights.shape[0]
    here = lax.axis_index("col").astype(jnp.int32).reshape(1)
    both = (0, 1)

    got1 = [None, None]
    for axis in ORDER:
        low, high = chunk_products(here, out_grads, activations, axis, (2,))
        got1[axis] = (send(low, axis, 1), send(high, axis, -1))
    near = together([chunk_products(here, out_grads, activations, axis, (1, -1)) for axis in both])
    got2, sent = [None, None], []
    for axis in ORDER:
        terms = [
            terms.at[1].set(add(terms[1], arrived).astype(bf16))
            for terms, arrived in zip(near[axis], got1[axis])
        ]
        got2[axis] = (send(terms[0], axis, 1), send(terms[1], axis, -1))
        sent += terms
    ready = after(here, *sent)
    own = [chunk_products(ready, out_grads, activations, axis, (0,)) for axis in both]
    reduced = []
    for axis in both:
        up, down = got2[axis]
        reduced.append(add(own[axis][0], up[1], down[0]))
        reduced.append(add(own[axis][1], down[1], up[0]))
    got4 = []
    for axis in both:
        low, high = reduced[2 * axis], reduced[2 * axis + 1]
        plus = jnp.stack([low[0], high[1]]).astype(bf16)
        minus = jnp.stack([high[0], low[2]]).astype(bf16)
        got4.append((send(plus, 1 - axis, 1), send(minus, 1 - axis, -1)))
    pieces = []
    for axis in both:
        low, high = reduced[2 * axis], reduced[2 * axis + 1]
        up, down = got4[axis]
        plus = add(low[1], up[0]).astype(bf16)
        minus = add(high[2], down[0]).astype(bf16)
        up5, down5 = send(plus, 1 - axis, 1), send(minus, 1 - axis, -1)
        pieces.append(add(low[3], up5, down[1]))
        pieces.append(add(high[3], down5, up[1]))
    gradient = jnp.concatenate(pieces, axis=2)

    param_squares = jnp.sum(weights * weights, axis=(1, 2))
    pure = gradient * gradient
    square = pure + square_eps
    stage = jnp.concatenate([jnp.sum(square, axis=2).reshape(-1), param_squares])
    stage = lax.psum(stage, "row")
    row_sum = stage[: mats * TILE].reshape(mats, TILE)
    param_part = stage[mats * TILE :]
    row_new = decay_rate * row_prev + (1.0 - decay_rate) * row_sum / D
    col_part = jnp.sum(square, axis=1)
    base = gradient * lax.rsqrt(row_new)[:, :, None]
    mix_part = jnp.sum(base * base, axis=1)
    scalars = jnp.concatenate([jnp.sum(row_new, axis=1), param_part])
    payload = jnp.concatenate(
        [
            col_part.reshape(-1, 128),
            mix_part.reshape(-1, 128),
            jnp.pad(scalars, (0, 8 * 128 - 2 * mats)).reshape(8, 128),
        ]
    )
    gathered = lax.all_to_all(
        jnp.broadcast_to(payload[None], (SIDE * SIDE,) + payload.shape), "col", 0, 0
    )
    total = jnp.sum(gathered, axis=0)
    lines = mats * 1024 // 128
    col_sum = total[:lines].reshape(mats, 1024)
    mix_sum = total[lines : 2 * lines].reshape(mats, 1024)
    row_mean = total[2 * lines, :mats] / INNER
    param_totals = total[2 * lines, mats : 2 * mats]
    col_new = decay_rate * col_prev + (1.0 - decay_rate) * col_sum / INNER
    scaled_total = lax.psum(jnp.sum(mix_sum / col_new, axis=1), "row") * row_mean
    entry_count = INNER * D
    update_scale = jnp.sqrt(scaled_total / entry_count + 1e-06)
    param_scale = jnp.sqrt(param_totals / entry_count + 1e-06)
    shrink = jnp.sqrt(row_mean) / jnp.maximum(1.0, update_scale / clip_limit)
    col_factor = lax.rsqrt(col_new) * shrink[:, None]
    clipped = base * col_factor[:, None, :]
    updated = weights - (step_scale * param_scale)[:, None, None] * clipped
    direction = clipped.astype(bf16)
    return updated, direction, row_new, col_new, update_scale, param_scale


def solution(mesh):
    placed = (
        P(("section", "col"), "row"),
        P(None, ("section", "col"), None),
        P("section", "col", "row"),
        P("section", "col"),
        P("section", "row"),
    )
    return jax.shard_map(
        body,
        mesh=mesh,
        in_specs=placed,
        out_specs=(
            P("section", "col", "row"),
            P("section", "col", "row"),
            P("section", "col"),
            P("section", "row"),
            P("section"),
            P("section"),
        ),
        check_vma=False,
    )
```

time: 167 us -> 154 us (0.922)
  starting transfers between devices: 35.7 us -> 23.4 us
  waiting for transfers between devices: 50.4 us -> 45.5 us
  blocking collectives: 32.2 us -> 36.7 us
    ppermute x24 -> x16, starting transfers between devices: 35.7 us -> 23.4 us  [send(): return lax.ppermute(value, 'col', shift_pairs(axis, step))]
    ppermute x24 -> x16, waiting for transfers between devices: 50.4 us -> 45.5 us  [send(): return lax.ppermute(value, 'col', shift_pairs(axis, step))]
    all_to_all x1, blocking collectives: 13.8 us -> 18.2 us  [body(): lax.all_to_all(jnp.broadcast_to(payload[None], (SIDE * SIDE,) + payload.s...]
    convert_element_type x13 -> x5, other arithmetic: 7.52 us -> 3.93 us  [the longest x1 3.68 us: body(): direction = clipped.astype(bf16)]
  transfers between devices with their start and end apart: 24 -> 16, of which waited for: 12 -> 9; matrix products, arithmetic and copies ran while one was open for 3% -> 3% of each run, Pallas kernels for 17% -> 19%
where the time goes in v2:
time: 154 us; the launch traced here: 152 us
  waiting for transfers between devices  45.5 us (30%)
  blocking collectives  36.7 us (24%)
  Pallas kernels  33 us (21%)
  starting transfers between devices  23.4 us (15%)
  other arithmetic  9.92 us (6%)
  local copies, waits for them, and re-layouts  2.12 us (1%)
    ppermute x16, waiting for transfers between devices, send(): return lax.ppermute(value, 'col', shift_pairs(axis, step))  45.5 us
    pallas_call x6, Pallas kernels, chunk_products(): pl.pallas_call(functools.partial(chunk_kernel, near), grid_spec=pltpu.Pre...  33 us
    ppermute x16, starting transfers between devices, send(): return lax.ppermute(value, 'col', shift_pairs(axis, step))  23.4 us
    all_to_all x1, blocking collectives, body(): lax.all_to_all(jnp.broadcast_to(payload[None], (SIDE * SIDE,) + payload.s...  18.2 us
    psum x1, blocking collectives, body(): stage = lax.psum(stage, 'row')  10.8 us
    psum x1, blocking collectives, body(): lax.psum(jnp.sum(mix_sum / col_new, axis=1), 'row') * row_mean  7.75 us
    convert_element_type x1, other arithmetic, body(): direction = clipped.astype(bf16)  3.68 us
  transfers between devices with their start and end apart: 16, of which 9 were waited for; matrix products, arithmetic and copies ran while one was open for 3% of the time, Pallas kernels for 19%

profile of v2, /device:TPU:32, one launch (start us, length us, event | category | flops | bytes accessed | tf_op | source)
XLA Modules:
  0.0 151.6 jit_solution(7575015153269367377)
XLA Ops:
  0.6 1.6 %copy-done = bf16[1024,1024]{1,0:T(8,128)(2,1)S(1)} copy-done((bf16[1024,1024]{1,0:T(8,128)(2,1)S(1)}, bf16[1024,1024]{1,0:T(8,128)(2,1)}, u32[]{:S(2)}) %copy-start) | copy-done | bytes 2097176
  2.2 4.3 %shard_map.103 = (bf16[4,2,256,256]{3,2,1,0:T(8,128)(2,1)S(1)}, bf16[4,2,256,256]{3,2,1,0:T(8,128)(2,1)S(1)}) custom-call(s32[1]{0:T(128)} %bitcast.here, bf16[2,1024,4096]{2,1,0:T(8,128)(2,1)} %d3.11, bf16[2,1024,4096]{2,1,0:T(8,128)(2,1)} %d3.11, bf16[2,1024,4096]{2,1,0:T(8,128)(2,1)} %d3.11, bf16[2,1024,4096]{2,1,0:T(8,128)(2,1)} %d3.11, ...), custom_call_target="tpu_custom_call" | custom-call | tf_op jit(solution)/shard_map/pallas_call | solution.py:71
  6.6 1.6 %collective-permute-start.2 = (bf16[4,2,256,256]{3,2,1,0:T(8,128)(2,1)S(1)}, bf16[4,2,256,256]{3,2,1,0:T(8,128)(2,1)S(1)}, u32[]{:S(2)}, u32[]{:S(2)}) collective-permute-start(bf16[4,2,256,256]{3,2,1,0:T(8,128)(2,1)S(1)} %get-tuple-element.80), channel_id=1, source_target_pairs={{0,4},{1,5},{2,6},{3,7},{4,8},{5,9},{6,10},{7,11},{8,12},{9,13},{1... | collective-permute-start | bytes 3145736 | tf_op jit(solution)/shard_map/ppermute | solution.py:95
  8.1 1.7 %collective-permute-start.3 = (bf16[4,2,256,256]{3,2,1,0:T(8,128)(2,1)S(1)}, bf16[4,2,256,256]{3,2,1,0:T(8,128)(2,1)S(1)}, u32[]{:S(2)}, u32[]{:S(2)}) collective-permute-start(bf16[4,2,256,256]{3,2,1,0:T(8,128)(2,1)S(1)} %get-tuple-element.82), channel_id=1, source_target_pairs={{0,12},{1,13},{2,14},{3,15},{4,0},{5,1},{6,2},{7,3},{8,4},{9,5},{1... | collective-permute-start | bytes 3145736 | tf_op jit(solution)/shard_map/ppermute | solution.py:95
  9.9 4.4 %shard_map.102 = (bf16[4,2,256,256]{3,2,1,0:T(8,128)(2,1)S(1)}, bf16[4,2,256,256]{3,2,1,0:T(8,128)(2,1)S(1)}) custom-call(s32[1]{0:T(128)} %bitcast.here, bf16[2,1024,4096]{2,1,0:T(8,128)(2,1)} %d3.11, bf16[2,1024,4096]{2,1,0:T(8,128)(2,1)} %d3.11, bf16[2,1024,4096]{2,1,0:T(8,128)(2,1)} %d3.11, bf16[2,1024,4096]{2,1,0:T(8,128)(2,1)} %d3.11, ...), custom_call_target="tpu_custom_call" | custom-call | tf_op jit(solution)/shard_map/pallas_call | solution.py:71
  14.2 2.0 %collective-permute-start = (bf16[4,2,256,256]{3,2,1,0:T(8,128)(2,1)S(1)}, bf16[4,2,256,256]{3,2,1,0:T(8,128)(2,1)S(1)}, u32[]{:S(2)}, u32[]{:S(2)}) collective-permute-start(bf16[4,2,256,256]{3,2,1,0:T(8,128)(2,1)S(1)} %get-tuple-element.76), channel_id=1, source_target_pairs={{0,1},{1,2},{2,3},{3,0},{4,5},{5,6},{6,7},{7,4},{8,9},{9,10},{10,1... | collective-permute-start | bytes 3145736 | tf_op jit(solution)/shard_map/ppermute | solution.py:95
  16.2 0.1 collective-permute-start.1
  16.3 7.7 %shard_map.100 = (bf16[2,4,2,256,256]{4,3,2,1,0:T(8,128)(2,1)S(1)}, bf16[2,4,2,256,256]{4,3,2,1,0:T(8,128)(2,1)S(1)}) custom-call(s32[1]{0:T(128)} %bitcast.here, bf16[2,1024,4096]{2,1,0:T(8,128)(2,1)} %d3.11, bf16[2,1024,4096]{2,1,0:T(8,128)(2,1)} %d3.11, bf16[2,1024,4096]{2,1,0:T(8,128)(2,1)} %d3.11, bf16[2,1024,4096]{2,1,0:T(8,128)(2,1)} %d3.11, ...), custom_call_target="tpu_custom_call" | custom-call | tf_op jit(solution)/shard_map/pallas_call | solution.py:71
  24.1 7.8 %shard_map.101 = (bf16[2,4,2,256,256]{4,3,2,1,0:T(8,128)(2,1)S(1)}, bf16[2,4,2,256,256]{4,3,2,1,0:T(8,128)(2,1)S(1)}) custom-call(s32[1]{0:T(128)} %bitcast.here, bf16[2,1024,4096]{2,1,0:T(8,128)(2,1)} %d3.11, bf16[2,1024,4096]{2,1,0:T(8,128)(2,1)} %d3.11, bf16[2,1024,4096]{2,1,0:T(8,128)(2,1)} %d3.11, bf16[2,1024,4096]{2,1,0:T(8,128)(2,1)} %d3.11, ...), custom_call_target="tpu_custom_call" | custom-call | tf_op jit(solution)/shard_map/pallas_call | solution.py:71
  31.9 0.1 slice.256
  32.0 0.1 slice.257
  32.1 0.7 collective-permute-done.2
  32.8 0.3 fusion.11
  33.1 0.3 collective-permute-start.4
  33.4 0.3 fusion.13
  33.7 3.0 %collective-permute-start.5 = (bf16[2,4,2,256,256]{4,3,2,1,0:T(8,128)(2,1)S(1)}, bf16[2,4,2,256,256]{4,3,2,1,0:T(8,128)(2,1)S(1)}, u32[]{:S(2)}, u32[]{:S(2)}) collective-permute-start(bf16[2,4,2,256,256]{4,3,2,1,0:T(8,128)(2,1)S(1)} %fusion.13), channel_id=1, source_target_pairs={{0,12},{1,13},{2,14},{3,15},{4,0},{5,1},{6,2},{7,3},{8,4},{9,5},{1... | collective-permute-start | bytes 6291464 | tf_op jit(solution)/shard_map/ppermute | solution.py:95
  36.8 0.1 slice.254
  36.8 0.1 slice.255
  36.9 1.8 %collective-permute-done = bf16[4,2,256,256]{3,2,1,0:T(8,128)(2,1)S(1)} collective-permute-done((bf16[4,2,256,256]{3,2,1,0:T(8,128)(2,1)S(1)}, bf16[4,2,256,256]{3,2,1,0:T(8,128)(2,1)S(1)}, u32[]{:S(2)}, u32[]{:S(2)}) %collective-permute-start) | collective-permute-done | bytes 1048608 | tf_op jit(solution)/shard_map/ppermute | solution.py:95
  38.7 0.3 fusion.7
  39.0 2.0 %collective-permute-start.10 = (bf16[2,4,2,256,256]{4,3,2,1,0:T(8,128)(2,1)S(1)}, bf16[2,4,2,256,256]{4,3,2,1,0:T(8,128)(2,1)S(1)}, u32[]{:S(2)}, u32[]{:S(2)}) collective-permute-start(bf16[2,4,2,256,256]{4,3,2,1,0:T(8,128)(2,1)S(1)} %fusion.7), channel_id=1, source_target_pairs={{0,1},{1,2},{2,3},{3,0},{4,5},{5,6},{6,7},{7,4},{8,9},{9,10},{10,1... | collective-permute-start | bytes 6291464 | tf_op jit(solution)/shard_map/ppermute | solution.py:95
  41.0 0.3 fusion.9
  41.3 0.8 collective-permute-start.11
  42.0 0.4 multiply_reduce_fusion.1
  42.4 4.4 %shard_map.104 = (bf16[4,2,256,256]{3,2,1,0:T(8,128)(2,1)S(1)}, bf16[4,2,256,256]{3,2,1,0:T(8,128)(2,1)S(1)}) custom-call(s32[1]{0:T(128)} %bitcast.here, bf16[2,1024,4096]{2,1,0:T(8,128)(2,1)} %d3.11, bf16[2,1024,4096]{2,1,0:T(8,128)(2,1)} %d3.11, bf16[2,1024,4096]{2,1,0:T(8,128)(2,1)} %d3.11, bf16[2,1024,4096]{2,1,0:T(8,128)(2,1)} %d3.11, ...), custom_call_target="tpu_custom_call" | custom-call | tf_op jit(solution)/shard_map/pallas_call | solution.py:71
  46.8 4.4 %shard_map.105 = (bf16[4,2,256,256]{3,2,1,0:T(8,128)(2,1)S(1)}, bf16[4,2,256,256]{3,2,1,0:T(8,128)(2,1)S(1)}) custom-call(s32[1]{0:T(128)} %bitcast.here, bf16[2,1024,4096]{2,1,0:T(8,128)(2,1)} %d3.11, bf16[2,1024,4096]{2,1,0:T(8,128)(2,1)} %d3.11, bf16[2,1024,4096]{2,1,0:T(8,128)(2,1)} %d3.11, bf16[2,1024,4096]{2,1,0:T(8,128)(2,1)} %d3.11, ...), custom_call_target="tpu_custom_call" | custom-call | tf_op jit(solution)/shard_map/pallas_call | solution.py:71
  51.2 29.6 %collective-permute-done.4 = bf16[2,4,2,256,256]{4,3,2,1,0:T(8,128)(2,1)S(1)} collective-permute-done((bf16[2,4,2,256,256]{4,3,2,1,0:T(8,128)(2,1)S(1)}, bf16[2,4,2,256,256]{4,3,2,1,0:T(8,128)(2,1)S(1)}, u32[]{:S(2)}, u32[]{:S(2)}) %collective-permute-start.4) | collective-permute-done | bytes 2097184 | tf_op jit(solution)/shard_map/ppermute | solution.py:95
  80.8 1.0 fusion.38
  81.9 0.1 fusion.41
  82.0 2.0 %collective-permute-start.6 = (bf16[2,2,256,256]{3,2,1,0:T(8,128)(2,1)S(1)}, bf16[2,2,256,256]{3,2,1,0:T(8,128)(2,1)S(1)}, u32[]{:S(2)}, u32[]{:S(2)}) collective-permute-start(bf16[2,2,256,256]{3,2,1,0:T(8,128)(2,1)S(1)} %pad_maximum_fusion.1), channel_id=1, source_target_pairs={{0,1},{1,2},{2,3},{3,0},{4,5},{5,6},{6,7},{7,4},{8,9},{9,10},{10,1... | collective-permute-start | bytes 1572872 | tf_op jit(solution)/shard_map/ppermute | solution.py:95
  84.1 0.2 collective-permute-start.8
  84.2 3.8 %collective-permute-done.10 = bf16[2,4,2,256,256]{4,3,2,1,0:T(8,128)(2,1)S(1)} collective-permute-done((bf16[2,4,2,256,256]{4,3,2,1,0:T(8,128)(2,1)S(1)}, bf16[2,4,2,256,256]{4,3,2,1,0:T(8,128)(2,1)S(1)}, u32[]{:S(2)}, u32[]{:S(2)}) %collective-permute-start.10) | collective-permute-done | bytes 2097184 | tf_op jit(solution)/shard_map/ppermute | solution.py:95
  88.0 1.7 %collective-permute-done.11 = bf16[2,4,2,256,256]{4,3,2,1,0:T(8,128)(2,1)S(1)} collective-permute-done((bf16[2,4,2,256,256]{4,3,2,1,0:T(8,128)(2,1)S(1)}, bf16[2,4,2,256,256]{4,3,2,1,0:T(8,128)(2,1)S(1)}, u32[]{:S(2)}, u32[]{:S(2)}) %collective-permute-start.11) | collective-permute-done | bytes 2097184 | tf_op jit(solution)/shard_map/ppermute | solution.py:95
  89.7 1.1 fusion.40
  90.8 0.1 fusion.43
  90.9 0.3 collective-permute-start.12
  91.2 3.1 %collective-permute-start.14 = (bf16[2,2,256,256]{3,2,1,0:T(8,128)(2,1)S(1)}, bf16[2,2,256,256]{3,2,1,0:T(8,128)(2,1)S(1)}, u32[]{:S(2)}, u32[]{:S(2)}) collective-permute-start(bf16[2,2,256,256]{3,2,1,0:T(8,128)(2,1)S(1)} %pad_maximum_fusion.4), channel_id=1, source_target_pairs={{0,12},{1,13},{2,14},{3,15},{4,0},{5,1},{6,2},{7,3},{8,4},{9,5},{1... | collective-permute-start | bytes 1572872 | tf_op jit(solution)/shard_map/ppermute | solution.py:95
  94.3 2.8 %collective-permute-done.6 = bf16[2,2,256,256]{3,2,1,0:T(8,128)(2,1)S(1)} collective-permute-done((bf16[2,2,256,256]{3,2,1,0:T(8,128)(2,1)S(1)}, bf16[2,2,256,256]{3,2,1,0:T(8,128)(2,1)S(1)}, u32[]{:S(2)}, u32[]{:S(2)}) %collective-permute-start.6) | collective-permute-done | bytes 524320 | tf_op jit(solution)/shard_map/ppermute | solution.py:95
  97.1 0.1 fusion.26
  97.2 1.0 collective-permute-start.7
  98.2 0.1 collective-permute-done.8
  98.4 0.1 fusion.27
  98.4 1.9 %collective-permute-start.9 = (bf16[2,256,256]{2,1,0:T(8,128)(2,1)S(1)}, bf16[2,256,256]{2,1,0:T(8,128)(2,1)S(1)}, u32[]{:S(2)}, u32[]{:S(2)}) collective-permute-start(bf16[2,256,256]{2,1,0:T(8,128)(2,1)S(1)} %fusion.27), channel_id=1, source_target_pairs={{0,3},{1,0},{2,1},{3,2},{4,7},{5,4},{6,5},{7,6},{8,11},{9,8},{10,9... | collective-permute-start | bytes 786440 | tf_op jit(solution)/shard_map/ppermute | solution.py:95
  100.4 1.0 collective-permute-done.12
  101.4 0.1 fusion.28
  101.4 0.1 collective-permute-start.13
  101.5 0.1 fusion.29
  101.6 3.3 %collective-permute-start.15 = (bf16[2,256,256]{2,1,0:T(8,128)(2,1)S(1)}, bf16[2,256,256]{2,1,0:T(8,128)(2,1)S(1)}, u32[]{:S(2)}, u32[]{:S(2)}) collective-permute-start(bf16[2,256,256]{2,1,0:T(8,128)(2,1)S(1)} %fusion.29), channel_id=1, source_target_pairs={{0,12},{1,13},{2,14},{3,15},{4,0},{5,1},{6,2},{7,3},{8,4},{9,5},{1... | collective-permute-start | bytes 786440 | tf_op jit(solution)/shard_map/ppermute | solution.py:95
  104.9 0.1 fusion.25
  105.0 0.1 fusion.22
  105.1 4.0 %collective-permute-done.13 = bf16[2,256,256]{2,1,0:T(8,128)(2,1)S(1)} collective-permute-done((bf16[2,256,256]{2,1,0:T(8,128)(2,1)S(1)}, bf16[2,256,256]{2,1,0:T(8,128)(2,1)S(1)}, u32[]{:S(2)}, u32[]{:S(2)}) %collective-permute-start.13) | collective-permute-done | bytes 262176 | tf_op jit(solution)/shard_map/ppermute | solution.py:95
  109.1 0.1 fusion.19
  109.2 0.1 fusion.16
  109.3 0.3 fusion.4
  109.6 10.8 %psum.14 = f32[514]{0:T(1024)S(1)} all-reduce(f32[514]{0:T(1024)S(1)} %pad_maximum_fusion.6), channel_id=1, replica_groups=mesh['section'=2,'row'=4,'col'=16] {'row'}, use_global_device_ids=true, to_apply=%region_3.0 | all-reduce | flops 514 | bytes 4112 | tf_op jit(solution)/shard_map/psum | solution.py:163
  120.4 0.5 fusion.5
  120.9 0.1 reduce_sum.67
  121.0 0.1 fusion.30
  121.1 18.2 %all_to_all.5 = f32[16,40,128]{2,1,0:T(8,128)S(1)} all-to-all(f32[16,40,128]{2,1,0:T(8,128)S(1)} %broadcast_in_dim.2), channel_id=1, replica_groups=mesh['section'=2,'row'=4,'col'=16] {'col'}, dimensions={0} | all-to-all | bytes 655360 | tf_op jit(solution)/shard_map/all_to_all | solution.py:178
  139.3 0.1 divide_reduce_fusion
  139.5 7.7 %psum.15 = f32[2]{0:T(128)S(1)} all-reduce(f32[2]{0:T(128)S(1)} %get-tuple-element.94), channel_id=1, replica_groups=mesh['section'=2,'row'=4,'col'=16] {'row'}, use_global_device_ids=true, to_apply=%region_8.0 | all-reduce | flops 2 | bytes 16 | tf_op jit(solution)/shard_map/psum | solution.py:188
  147.2 0.6 broadcast_multiply_fusion
  147.8 0.1 rsqrt_multiply_fusion
  147.9 3.7 %multiply_convert_fusion = (bf16[2,256,1024]{2,1,0:T(8,128)(2,1)}, f32[2,256,1024]{2,1,0:T(8,128)}) fusion(f32[2,1024]{1,0:T(2,128)S(1)} %rsqrt_multiply_fusion, f32[2,256]{1,0:T(2,128)S(1)} %get-tuple-element.96, f32[2,256,256]{2,1,0:T(8,128)S(1)} %fusion.16, f32[2,256,256]{2,1,0:T(8,128)S(1)} %fusion.19, f32[2,256,256]{2,1,0:T(8,128)S(1)} %fusion.22, ...), kind=kLoop, calls=%fused_computation.21 | loop fusion | flops 4194304 | bytes 7350280 | tf_op jit(solution)/shard_map/convert_element_type | solution.py:196
  (36 shorter events, 0.4 us)
Async XLA Ops:
  0.6 1.6 %copy-start = (bf16[1024,1024]{1,0:T(8,128)(2,1)S(1)}, bf16[1024,1024]{1,0:T(8,128)(2,1)}, u32[]{:S(2)}) copy-start(bf16[1024,1024]{1,0:T(8,128)(2,1)} %x_ref.11) | copy-start | bytes 6291460
  6.6 26.2 %collective-permute-start.2 = (bf16[4,2,256,256]{3,2,1,0:T(8,128)(2,1)S(1)}, bf16[4,2,256,256]{3,2,1,0:T(8,128)(2,1)S(1)}, u32[]{:S(2)}, u32[]{:S(2)}) collective-permute-start(bf16[4,2,256,256]{3,2,1,0:T(8,128)(2,1)S(1)} %get-tuple-element.80), channel_id=1, source_target_pairs={{0,4},{1,5},{2,6},{3,7},{4,8},{5,9},{6,10},{7,11},{8,12},{9,13},{1... | collective-permute-start | bytes 3145736 | tf_op jit(solution)/shard_map/ppermute | solution.py:95
  8.1 25.3 %collective-permute-start.3 = (bf16[4,2,256,256]{3,2,1,0:T(8,128)(2,1)S(1)}, bf16[4,2,256,256]{3,2,1,0:T(8,128)(2,1)S(1)}, u32[]{:S(2)}, u32[]{:S(2)}) collective-permute-start(bf16[4,2,256,256]{3,2,1,0:T(8,128)(2,1)S(1)} %get-tuple-element.82), channel_id=1, source_target_pairs={{0,12},{1,13},{2,14},{3,15},{4,0},{5,1},{6,2},{7,3},{8,4},{9,5},{1... | collective-permute-start | bytes 3145736 | tf_op jit(solution)/shard_map/ppermute | solution.py:95
  14.2 24.4 %collective-permute-start = (bf16[4,2,256,256]{3,2,1,0:T(8,128)(2,1)S(1)}, bf16[4,2,256,256]{3,2,1,0:T(8,128)(2,1)S(1)}, u32[]{:S(2)}, u32[]{:S(2)}) collective-permute-start(bf16[4,2,256,256]{3,2,1,0:T(8,128)(2,1)S(1)} %get-tuple-element.76), channel_id=1, source_target_pairs={{0,1},{1,2},{2,3},{3,0},{4,5},{5,6},{6,7},{7,4},{8,9},{9,10},{10,1... | collective-permute-start | bytes 3145736 | tf_op jit(solution)/shard_map/ppermute | solution.py:95
  16.2 24.7 %collective-permute-start.1 = (bf16[4,2,256,256]{3,2,1,0:T(8,128)(2,1)S(1)}, bf16[4,2,256,256]{3,2,1,0:T(8,128)(2,1)S(1)}, u32[]{:S(2)}, u32[]{:S(2)}) collective-permute-start(bf16[4,2,256,256]{3,2,1,0:T(8,128)(2,1)S(1)} %get-tuple-element.78), channel_id=1, source_target_pairs={{0,3},{1,0},{2,1},{3,2},{4,7},{5,4},{6,5},{7,6},{8,11},{9,8},{10,9... | collective-permute-start | bytes 3145736 | tf_op jit(solution)/shard_map/ppermute | solution.py:95
  33.1 47.8 %collective-permute-start.4 = (bf16[2,4,2,256,256]{4,3,2,1,0:T(8,128)(2,1)S(1)}, bf16[2,4,2,256,256]{4,3,2,1,0:T(8,128)(2,1)S(1)}, u32[]{:S(2)}, u32[]{:S(2)}) collective-permute-start(bf16[2,4,2,256,256]{4,3,2,1,0:T(8,128)(2,1)S(1)} %fusion.11), channel_id=1, source_target_pairs={{0,4},{1,5},{2,6},{3,7},{4,8},{5,9},{6,10},{7,11},{8,12},{9,13},{1... | collective-permute-start | bytes 6291464 | tf_op jit(solution)/shard_map/ppermute | solution.py:95
  33.7 47.1 %collective-permute-start.5 = (bf16[2,4,2,256,256]{4,3,2,1,0:T(8,128)(2,1)S(1)}, bf16[2,4,2,256,256]{4,3,2,1,0:T(8,128)(2,1)S(1)}, u32[]{:S(2)}, u32[]{:S(2)}) collective-permute-start(bf16[2,4,2,256,256]{4,3,2,1,0:T(8,128)(2,1)S(1)} %fusion.13), channel_id=1, source_target_pairs={{0,12},{1,13},{2,14},{3,15},{4,0},{5,1},{6,2},{7,3},{8,4},{9,5},{1... | collective-permute-start | bytes 6291464 | tf_op jit(solution)/shard_map/ppermute | solution.py:95
  39.0 3.1 %copy-start.1 = (f32[2,256,1024]{2,1,0:T(8,128)S(1)}, f32[2,256,1024]{2,1,0:T(8,128)}, u32[]{:S(2)}) copy-start(f32[2,256,1024]{2,1,0:T(8,128)} %param.15) | copy-start | bytes 6291460
  39.0 49.0 %collective-permute-start.10 = (bf16[2,4,2,256,256]{4,3,2,1,0:T(8,128)(2,1)S(1)}, bf16[2,4,2,256,256]{4,3,2,1,0:T(8,128)(2,1)S(1)}, u32[]{:S(2)}, u32[]{:S(2)}) collective-permute-start(bf16[2,4,2,256,256]{4,3,2,1,0:T(8,128)(2,1)S(1)} %fusion.7), channel_id=1, source_target_pairs={{0,1},{1,2},{2,3},{3,0},{4,5},{5,6},{6,7},{7,4},{8,9},{9,10},{10,1... | collective-permute-start | bytes 6291464 | tf_op jit(solution)/shard_map/ppermute | solution.py:95
  41.3 48.4 %collective-permute-start.11 = (bf16[2,4,2,256,256]{4,3,2,1,0:T(8,128)(2,1)S(1)}, bf16[2,4,2,256,256]{4,3,2,1,0:T(8,128)(2,1)S(1)}, u32[]{:S(2)}, u32[]{:S(2)}) collective-permute-start(bf16[2,4,2,256,256]{4,3,2,1,0:T(8,128)(2,1)S(1)} %fusion.9), channel_id=1, source_target_pairs={{0,3},{1,0},{2,1},{3,2},{4,7},{5,4},{6,5},{7,6},{8,11},{9,8},{10,9... | collective-permute-start | bytes 6291464 | tf_op jit(solution)/shard_map/ppermute | solution.py:95
  82.0 15.1 %collective-permute-start.6 = (bf16[2,2,256,256]{3,2,1,0:T(8,128)(2,1)S(1)}, bf16[2,2,256,256]{3,2,1,0:T(8,128)(2,1)S(1)}, u32[]{:S(2)}, u32[]{:S(2)}) collective-permute-start(bf16[2,2,256,256]{3,2,1,0:T(8,128)(2,1)S(1)} %pad_maximum_fusion.1), channel_id=1, source_target_pairs={{0,1},{1,2},{2,3},{3,0},{4,5},{5,6},{6,7},{7,4},{8,9},{9,10},{10,1... | collective-permute-start | bytes 1572872 | tf_op jit(solution)/shard_map/ppermute | solution.py:95
  84.1 14.3 %collective-permute-start.8 = (bf16[2,2,256,256]{3,2,1,0:T(8,128)(2,1)S(1)}, bf16[2,2,256,256]{3,2,1,0:T(8,128)(2,1)S(1)}, u32[]{:S(2)}, u32[]{:S(2)}) collective-permute-start(bf16[2,2,256,256]{3,2,1,0:T(8,128)(2,1)S(1)} %pad_maximum_fusion.2), channel_id=1, source_target_pairs={{0,3},{1,0},{2,1},{3,2},{4,7},{5,4},{6,5},{7,6},{8,11},{9,8},{10,9... | collective-permute-start | bytes 1572872 | tf_op jit(solution)/shard_map/ppermute | solution.py:95
  90.9 10.5 %collective-permute-start.12 = (bf16[2,2,256,256]{3,2,1,0:T(8,128)(2,1)S(1)}, bf16[2,2,256,256]{3,2,1,0:T(8,128)(2,1)S(1)}, u32[]{:S(2)}, u32[]{:S(2)}) collective-permute-start(bf16[2,2,256,256]{3,2,1,0:T(8,128)(2,1)S(1)} %pad_maximum_fusion.3), channel_id=1, source_target_pairs={{0,4},{1,5},{2,6},{3,7},{4,8},{5,9},{6,10},{7,11},{8,12},{9,13},{1... | collective-permute-start | bytes 1572872 | tf_op jit(solution)/shard_map/ppermute | solution.py:95
  91.2 10.3 %collective-permute-start.14 = (bf16[2,2,256,256]{3,2,1,0:T(8,128)(2,1)S(1)}, bf16[2,2,256,256]{3,2,1,0:T(8,128)(2,1)S(1)}, u32[]{:S(2)}, u32[]{:S(2)}) collective-permute-start(bf16[2,2,256,256]{3,2,1,0:T(8,128)(2,1)S(1)} %pad_maximum_fusion.4), channel_id=1, source_target_pairs={{0,12},{1,13},{2,14},{3,15},{4,0},{5,1},{6,2},{7,3},{8,4},{9,5},{1... | collective-permute-start | bytes 1572872 | tf_op jit(solution)/shard_map/ppermute | solution.py:95
  97.2 7.7 %collective-permute-start.7 = (bf16[2,256,256]{2,1,0:T(8,128)(2,1)S(1)}, bf16[2,256,256]{2,1,0:T(8,128)(2,1)S(1)}, u32[]{:S(2)}, u32[]{:S(2)}) collective-permute-start(bf16[2,256,256]{2,1,0:T(8,128)(2,1)S(1)} %fusion.26), channel_id=1, source_target_pairs={{0,1},{1,2},{2,3},{3,0},{4,5},{5,6},{6,7},{7,4},{8,9},{9,10},{10,1... | collective-permute-start | bytes 786440 | tf_op jit(solution)/shard_map/ppermute | solution.py:95
  98.4 6.5 %collective-permute-start.9 = (bf16[2,256,256]{2,1,0:T(8,128)(2,1)S(1)}, bf16[2,256,256]{2,1,0:T(8,128)(2,1)S(1)}, u32[]{:S(2)}, u32[]{:S(2)}) collective-permute-start(bf16[2,256,256]{2,1,0:T(8,128)(2,1)S(1)} %fusion.27), channel_id=1, source_target_pairs={{0,3},{1,0},{2,1},{3,2},{4,7},{5,4},{6,5},{7,6},{8,11},{9,8},{10,9... | collective-permute-start | bytes 786440 | tf_op jit(solution)/shard_map/ppermute | solution.py:95
  101.4 7.7 %collective-permute-start.13 = (bf16[2,256,256]{2,1,0:T(8,128)(2,1)S(1)}, bf16[2,256,256]{2,1,0:T(8,128)(2,1)S(1)}, u32[]{:S(2)}, u32[]{:S(2)}) collective-permute-start(bf16[2,256,256]{2,1,0:T(8,128)(2,1)S(1)} %fusion.28), channel_id=1, source_target_pairs={{0,4},{1,5},{2,6},{3,7},{4,8},{5,9},{6,10},{7,11},{8,12},{9,13},{1... | collective-permute-start | bytes 786440 | tf_op jit(solution)/shard_map/ppermute | solution.py:95
  101.6 7.6 %collective-permute-start.15 = (bf16[2,256,256]{2,1,0:T(8,128)(2,1)S(1)}, bf16[2,256,256]{2,1,0:T(8,128)(2,1)S(1)}, u32[]{:S(2)}, u32[]{:S(2)}) collective-permute-start(bf16[2,256,256]{2,1,0:T(8,128)(2,1)S(1)} %fusion.29), channel_id=1, source_target_pairs={{0,12},{1,13},{2,14},{3,15},{4,0},{5,1},{6,2},{7,3},{8,4},{9,5},{1... | collective-permute-start | bytes 786440 | tf_op jit(solution)/shard_map/ppermute | solution.py:95
  109.2 11.2 %copy-start.5 = (f32[2,256]{1,0:T(2,128)S(1)}, f32[2,256]{1,0:T(2,128)}, u32[]{:S(2)}) copy-start(f32[2,256]{1,0:T(2,128)} %param.16) | copy-start | bytes 6148
  109.5 29.8 %copy-start.4 = (f32[2,1024]{1,0:T(2,128)S(1)}, f32[2,1024]{1,0:T(2,128)}, u32[]{:S(2)}) copy-start(f32[2,1024]{1,0:T(2,128)} %param.17) | copy-start | bytes 24580
  120.4 31.2 %copy-start.3 = (f32[2,256]{1,0:T(2,128)}, f32[2,256]{1,0:T(2,128)S(1)}, u32[]{:S(2)}) copy-start(f32[2,256]{1,0:T(2,128)S(1)} %get-tuple-element.97) | copy-start | bytes 6148
  139.5 12.1 %copy-start.2 = (f32[2,1024]{1,0:T(2,128)}, f32[2,1024]{1,0:T(2,128)S(1)}, u32[]{:S(2)}) copy-start(f32[2,1024]{1,0:T(2,128)S(1)} %get-tuple-element.95) | copy-start | bytes 24580

commit v3 on v2

--- a/solution.py
+++ b/solution.py
@@ -44,12 +44,10 @@
         store(targets[1], upper)
 
 
-def feature_block(here, axis, offset, part):
-    along = here >> 2 if axis == 0 else here
-    across = here if axis == 0 else here >> 2
-    along = (along + offset) & 3
-    across = (across + OTHER[part]) & 3
-    return along * SIDE + across if axis == 0 else across * SIDE + along
+def feature_block(table, axis, offset, part):
+    along = (table[axis] + offset) & 3
+    across = (table[1 - axis] + OTHER[part]) & 3
+    return along * table[2 + axis] + across * table[3 - axis]
 
 
 def chunk_products(here, out_grads, activations, axis, offsets):
@@ -59,7 +57,7 @@
     def block_spec(part):
         def index(m, c, t):
             offset = jnp.where(c == 0, offsets[0], offsets[1]) if near else offsets[0]
-            return (m, 0, feature_block(t[0], axis, offset, part))
+            return (m, 0, feature_block(t, axis, offset, part))
 
         return pl.BlockSpec((1, tokens, TILE), index)
 
@@ -84,23 +82,22 @@
 
 def shift_pairs(axis, step):
     pairs = []
-    for x in range(SIDE):
-        for z in range(SIDE):
-            to = ((x + step) % SIDE, z) if axis == 0 else (x, (z + step) % SIDE)
-            pairs.append((x * SIDE + z, to[0] * SIDE + to[1]))
+    for section in (0, 1):
+        for x in range(SIDE):
+            for z in range(SIDE):
+                along_x = axis == section
+                to = ((x + step) % SIDE, z) if along_x else (x, (z + step) % SIDE)
+                base = section * SIDE * SIDE
+                pairs.append((base + x * SIDE + z, base + to[0] * SIDE + to[1]))
     return pairs
 
 
 def send(value, axis, step):
-    return lax.ppermute(value, "col", shift_pairs(axis, step))
+    return lax.ppermute(value, ("section", "col"), shift_pairs(axis, step))
 
 
 def after(value, *others):
     return lax.optimization_barrier((value,) + others)[0]
-
-
-def together(values):
-    return lax.optimization_barrier(values)
 
 
 def add(*values):
@@ -111,19 +108,24 @@
 
 
 OTHER = (2, 1, 3, 0)
-ORDER = (1, 0)
+ORDER = (0, 1)
 
 
 def body(activations, out_grads, weights, row_prev, col_prev):
     mats = weights.shape[0]
-    here = lax.axis_index("col").astype(jnp.int32).reshape(1)
+    section = lax.axis_index("section").astype(jnp.int32)
+    col = lax.axis_index("col").astype(jnp.int32)
+    x, z, stride = col >> 2, col & 3, jnp.where(section == 0, SIDE, 1)
+    here = jnp.stack(
+        [jnp.where(section == 0, x, z), jnp.where(section == 0, z, x), stride, SIDE + 1 - stride]
+    )
     both = (0, 1)
 
     got1 = [None, None]
     for axis in ORDER:
         low, high = chunk_products(here, out_grads, activations, axis, (2,))
         got1[axis] = (send(low, axis, 1), send(high, axis, -1))
-    near = together([chunk_products(here, out_grads, activations, axis, (1, -1)) for axis in both])
+    near = [chunk_products(here, out_grads, activations, axis, (1, -1)) for axis in both]
     got2, sent = [None, None], []
     for axis in ORDER:
         terms = [

time: 154 us -> 141 us (0.916)
  waiting for transfers between devices: 45.5 us -> 33 us
  blocking collectives: 36.7 us -> 33.1 us
  Pallas kernels: 33 us -> 36.4 us
    ppermute x16, waiting for transfers between devices: 45.5 us -> 33 us  [send(): return lax.ppermute(value, ('section', 'col'), shift_pairs(axis, step))]
    all_to_all x1, blocking collectives: 18.2 us -> 14.6 us  [body(): lax.all_to_all(jnp.broadcast_to(payload[None], (SIDE * SIDE,) + payload.s...]
    pallas_call x6, Pallas kernels: 33 us -> 36.4 us  [chunk_products(): pl.pallas_call(functools.partial(chunk_kernel, near), grid_spec=pltpu.Pre...]
  transfers between devices with their start and end apart: 16 -> 16, of which waited for: 9 -> 10; matrix products, arithmetic and copies ran while one was open for 3% -> 3% of each run, Pallas kernels for 19% -> 23%
where the time goes in v3:
time: 141 us; the launch traced here: 139 us
  Pallas kernels  36.4 us (26%)
  blocking collectives  33.1 us (23%)
  waiting for transfers between devices  33 us (23%)
  starting transfers between devices  23.5 us (17%)
  other arithmetic  9.88 us (7%)
  local copies, waits for them, and re-layouts  2.13 us (2%)
    pallas_call x6, Pallas kernels, chunk_products(): pl.pallas_call(functools.partial(chunk_kernel, near), grid_spec=pltpu.Pre...  36.4 us
    ppermute x16, waiting for transfers between devices, send(): return lax.ppermute(value, ('section', 'col'), shift_pairs(axis, step))  33 us
    ppermute x16, starting transfers between devices, send(): return lax.ppermute(value, ('section', 'col'), shift_pairs(axis, step))  23.5 us
    all_to_all x1, blocking collectives, body(): lax.all_to_all(jnp.broadcast_to(payload[None], (SIDE * SIDE,) + payload.s...  14.6 us
    psum x1, blocking collectives, body(): stage = lax.psum(stage, 'row')  10.8 us
    psum x1, blocking collectives, body(): lax.psum(jnp.sum(mix_sum / col_new, axis=1), 'row') * row_mean  7.75 us
    convert_element_type x1, other arithmetic, body(): direction = clipped.astype(bf16)  3.68 us
  transfers between devices with their start and end apart: 16, of which 10 were waited for; matrix products, arithmetic and copies ran while one was open for 3% of the time, Pallas kernels for 23%

profile of v3, /device:TPU:32, one launch (start us, length us, event | category | flops | bytes accessed | tf_op | source)
XLA Modules:
  0.0 138.9 jit_solution(14217574620776105490)
XLA Ops:
  0.6 0.1 pad_add_fusion.here
  0.7 1.6 %copy-done = bf16[1024,1024]{1,0:T(8,128)(2,1)S(1)} copy-done((bf16[1024,1024]{1,0:T(8,128)(2,1)S(1)}, bf16[1024,1024]{1,0:T(8,128)(2,1)}, u32[]{:S(2)}) %copy-start) | copy-done | bytes 2097176
  2.3 4.9 %shard_map.101 = (bf16[4,2,256,256]{3,2,1,0:T(8,128)(2,1)S(1)}, bf16[4,2,256,256]{3,2,1,0:T(8,128)(2,1)S(1)}) custom-call(s32[4]{0:T(128)S(1)} %pad_add_fusion.here, bf16[2,1024,4096]{2,1,0:T(8,128)(2,1)} %d3.11, bf16[2,1024,4096]{2,1,0:T(8,128)(2,1)} %d3.11, bf16[2,1024,4096]{2,1,0:T(8,128)(2,1)} %d3.11, bf16[2,1024,4096]{2,1,0:T(8,128)(2,1)} %d3.11, ...), custom_call_target="tpu_custom_call" | custom-call | tf_op jit(solution)/shard_map/pallas_call | solution.py:69
  7.2 1.6 %collective-permute-start = (bf16[4,2,256,256]{3,2,1,0:T(8,128)(2,1)S(1)}, bf16[4,2,256,256]{3,2,1,0:T(8,128)(2,1)S(1)}, u32[]{:S(2)}, u32[]{:S(2)}) collective-permute-start(bf16[4,2,256,256]{3,2,1,0:T(8,128)(2,1)S(1)} %get-tuple-element.68), channel_id=1, source_target_pairs={{0,4},{1,5},{2,6},{3,7},{4,8},{5,9},{6,10},{7,11},{8,12},{9,13},{1... | collective-permute-start | bytes 3145736 | tf_op jit(solution)/shard_map/ppermute | solution.py:96
  8.8 1.7 %collective-permute-start.1 = (bf16[4,2,256,256]{3,2,1,0:T(8,128)(2,1)S(1)}, bf16[4,2,256,256]{3,2,1,0:T(8,128)(2,1)S(1)}, u32[]{:S(2)}, u32[]{:S(2)}) collective-permute-start(bf16[4,2,256,256]{3,2,1,0:T(8,128)(2,1)S(1)} %get-tuple-element.70), channel_id=1, source_target_pairs={{0,12},{1,13},{2,14},{3,15},{4,0},{5,1},{6,2},{7,3},{8,4},{9,5},{1... | collective-permute-start | bytes 3145736 | tf_op jit(solution)/shard_map/ppermute | solution.py:96
  10.6 4.9 %shard_map.103 = (bf16[4,2,256,256]{3,2,1,0:T(8,128)(2,1)S(1)}, bf16[4,2,256,256]{3,2,1,0:T(8,128)(2,1)S(1)}) custom-call(s32[4]{0:T(128)S(1)} %pad_add_fusion.here, bf16[2,1024,4096]{2,1,0:T(8,128)(2,1)} %d3.11, bf16[2,1024,4096]{2,1,0:T(8,128)(2,1)} %d3.11, bf16[2,1024,4096]{2,1,0:T(8,128)(2,1)} %d3.11, bf16[2,1024,4096]{2,1,0:T(8,128)(2,1)} %d3.11, ...), custom_call_target="tpu_custom_call" | custom-call | tf_op jit(solution)/shard_map/pallas_call | solution.py:69
  15.5 2.0 %collective-permute-start.2 = (bf16[4,2,256,256]{3,2,1,0:T(8,128)(2,1)S(1)}, bf16[4,2,256,256]{3,2,1,0:T(8,128)(2,1)S(1)}, u32[]{:S(2)}, u32[]{:S(2)}) collective-permute-start(bf16[4,2,256,256]{3,2,1,0:T(8,128)(2,1)S(1)} %get-tuple-element.72), channel_id=1, source_target_pairs={{0,1},{1,2},{2,3},{3,0},{4,5},{5,6},{6,7},{7,4},{8,9},{9,10},{10,1... | collective-permute-start | bytes 3145736 | tf_op jit(solution)/shard_map/ppermute | solution.py:96
  17.5 0.1 collective-permute-start.3
  17.6 8.3 %shard_map.100 = (bf16[2,4,2,256,256]{4,3,2,1,0:T(8,128)(2,1)S(1)}, bf16[2,4,2,256,256]{4,3,2,1,0:T(8,128)(2,1)S(1)}) custom-call(s32[4]{0:T(128)S(1)} %pad_add_fusion.here, bf16[2,1024,4096]{2,1,0:T(8,128)(2,1)} %d3.11, bf16[2,1024,4096]{2,1,0:T(8,128)(2,1)} %d3.11, bf16[2,1024,4096]{2,1,0:T(8,128)(2,1)} %d3.11, bf16[2,1024,4096]{2,1,0:T(8,128)(2,1)} %d3.11, ...), custom_call_target="tpu_custom_call" | custom-call | tf_op jit(solution)/shard_map/pallas_call | solution.py:69
  25.9 0.1 slice.254
  26.0 0.1 slice.255
  26.1 2.9 %collective-permute-done = bf16[4,2,256,256]{3,2,1,0:T(8,128)(2,1)S(1)} collective-permute-done((bf16[4,2,256,256]{3,2,1,0:T(8,128)(2,1)S(1)}, bf16[4,2,256,256]{3,2,1,0:T(8,128)(2,1)S(1)}, u32[]{:S(2)}, u32[]{:S(2)}) %collective-permute-start) | collective-permute-done | bytes 1048608 | tf_op jit(solution)/shard_map/ppermute | solution.py:96
  29.0 0.3 fusion.7
  29.3 0.3 collective-permute-start.4
  29.6 0.3 fusion.9
  29.9 3.0 %collective-permute-start.5 = (bf16[2,4,2,256,256]{4,3,2,1,0:T(8,128)(2,1)S(1)}, bf16[2,4,2,256,256]{4,3,2,1,0:T(8,128)(2,1)S(1)}, u32[]{:S(2)}, u32[]{:S(2)}) collective-permute-start(bf16[2,4,2,256,256]{4,3,2,1,0:T(8,128)(2,1)S(1)} %fusion.9), channel_id=1, source_target_pairs={{0,12},{1,13},{2,14},{3,15},{4,0},{5,1},{6,2},{7,3},{8,4},{9,5},{1... | collective-permute-start | bytes 6291464 | tf_op jit(solution)/shard_map/ppermute | solution.py:96
  32.9 8.3 %shard_map.102 = (bf16[2,4,2,256,256]{4,3,2,1,0:T(8,128)(2,1)S(1)}, bf16[2,4,2,256,256]{4,3,2,1,0:T(8,128)(2,1)S(1)}) custom-call(s32[4]{0:T(128)S(1)} %pad_add_fusion.here, bf16[2,1024,4096]{2,1,0:T(8,128)(2,1)} %d3.11, bf16[2,1024,4096]{2,1,0:T(8,128)(2,1)} %d3.11, bf16[2,1024,4096]{2,1,0:T(8,128)(2,1)} %d3.11, bf16[2,1024,4096]{2,1,0:T(8,128)(2,1)} %d3.11, ...), custom_call_target="tpu_custom_call" | custom-call | tf_op jit(solution)/shard_map/pallas_call | solution.py:69
  41.3 0.1 slice.256
  41.4 0.1 slice.257
  41.5 0.3 fusion.11
  41.8 2.2 %collective-permute-start.10 = (bf16[2,4,2,256,256]{4,3,2,1,0:T(8,128)(2,1)S(1)}, bf16[2,4,2,256,256]{4,3,2,1,0:T(8,128)(2,1)S(1)}, u32[]{:S(2)}, u32[]{:S(2)}) collective-permute-start(bf16[2,4,2,256,256]{4,3,2,1,0:T(8,128)(2,1)S(1)} %fusion.11), channel_id=1, source_target_pairs={{0,1},{1,2},{2,3},{3,0},{4,5},{5,6},{6,7},{7,4},{8,9},{9,10},{10,1... | collective-permute-start | bytes 6291464 | tf_op jit(solution)/shard_map/ppermute | solution.py:96
  43.9 0.3 fusion.13
  44.2 0.3 collective-permute-start.11
  44.5 0.4 multiply_reduce_fusion.1
  44.9 4.9 %shard_map.104 = (bf16[4,2,256,256]{3,2,1,0:T(8,128)(2,1)S(1)}, bf16[4,2,256,256]{3,2,1,0:T(8,128)(2,1)S(1)}) custom-call(s32[4]{0:T(128)S(1)} %pad_add_fusion.here, bf16[2,1024,4096]{2,1,0:T(8,128)(2,1)} %d3.11, bf16[2,1024,4096]{2,1,0:T(8,128)(2,1)} %d3.11, bf16[2,1024,4096]{2,1,0:T(8,128)(2,1)} %d3.11, bf16[2,1024,4096]{2,1,0:T(8,128)(2,1)} %d3.11, ...), custom_call_target="tpu_custom_call" | custom-call | tf_op jit(solution)/shard_map/pallas_call | solution.py:69
  49.8 4.9 %shard_map.105 = (bf16[4,2,256,256]{3,2,1,0:T(8,128)(2,1)S(1)}, bf16[4,2,256,256]{3,2,1,0:T(8,128)(2,1)S(1)}) custom-call(s32[4]{0:T(128)S(1)} %pad_add_fusion.here, bf16[2,1024,4096]{2,1,0:T(8,128)(2,1)} %d3.11, bf16[2,1024,4096]{2,1,0:T(8,128)(2,1)} %d3.11, bf16[2,1024,4096]{2,1,0:T(8,128)(2,1)} %d3.11, bf16[2,1024,4096]{2,1,0:T(8,128)(2,1)} %d3.11, ...), custom_call_target="tpu_custom_call" | custom-call | tf_op jit(solution)/shard_map/pallas_call | solution.py:69
  54.8 18.8 %collective-permute-done.4 = bf16[2,4,2,256,256]{4,3,2,1,0:T(8,128)(2,1)S(1)} collective-permute-done((bf16[2,4,2,256,256]{4,3,2,1,0:T(8,128)(2,1)S(1)}, bf16[2,4,2,256,256]{4,3,2,1,0:T(8,128)(2,1)S(1)}, u32[]{:S(2)}, u32[]{:S(2)}) %collective-permute-start.4) | collective-permute-done | bytes 2097184 | tf_op jit(solution)/shard_map/ppermute | solution.py:96
  73.5 0.5 collective-permute-done.5
  74.0 1.0 fusion.38
  75.1 0.1 fusion.41
  75.2 2.9 %collective-permute-start.6 = (bf16[2,2,256,256]{3,2,1,0:T(8,128)(2,1)S(1)}, bf16[2,2,256,256]{3,2,1,0:T(8,128)(2,1)S(1)}, u32[]{:S(2)}, u32[]{:S(2)}) collective-permute-start(bf16[2,2,256,256]{3,2,1,0:T(8,128)(2,1)S(1)} %pad_maximum_fusion.1), channel_id=1, source_target_pairs={{0,1},{1,2},{2,3},{3,0},{4,5},{5,6},{6,7},{7,4},{8,9},{9,10},{10,1... | collective-permute-start | bytes 1572872 | tf_op jit(solution)/shard_map/ppermute | solution.py:96
  78.1 0.1 collective-permute-start.8
  78.2 0.6 collective-permute-done.11
  78.8 1.0 fusion.40
  79.8 0.1 fusion.43
  80.0 1.6 %collective-permute-start.12 = (bf16[2,2,256,256]{3,2,1,0:T(8,128)(2,1)S(1)}, bf16[2,2,256,256]{3,2,1,0:T(8,128)(2,1)S(1)}, u32[]{:S(2)}, u32[]{:S(2)}) collective-permute-start(bf16[2,2,256,256]{3,2,1,0:T(8,128)(2,1)S(1)} %pad_maximum_fusion.3), channel_id=1, source_target_pairs={{0,4},{1,5},{2,6},{3,7},{4,8},{5,9},{6,10},{7,11},{8,12},{9,13},{1... | collective-permute-start | bytes 1572872 | tf_op jit(solution)/shard_map/ppermute | solution.py:96
  81.6 1.8 %collective-permute-start.14 = (bf16[2,2,256,256]{3,2,1,0:T(8,128)(2,1)S(1)}, bf16[2,2,256,256]{3,2,1,0:T(8,128)(2,1)S(1)}, u32[]{:S(2)}, u32[]{:S(2)}) collective-permute-start(bf16[2,2,256,256]{3,2,1,0:T(8,128)(2,1)S(1)} %pad_maximum_fusion.4), channel_id=1, source_target_pairs={{0,12},{1,13},{2,14},{3,15},{4,0},{5,1},{6,2},{7,3},{8,4},{9,5},{1... | collective-permute-start | bytes 1572872 | tf_op jit(solution)/shard_map/ppermute | solution.py:96
  83.4 2.9 %collective-permute-done.6 = bf16[2,2,256,256]{3,2,1,0:T(8,128)(2,1)S(1)} collective-permute-done((bf16[2,2,256,256]{3,2,1,0:T(8,128)(2,1)S(1)}, bf16[2,2,256,256]{3,2,1,0:T(8,128)(2,1)S(1)}, u32[]{:S(2)}, u32[]{:S(2)}) %collective-permute-start.6) | collective-permute-done | bytes 524320 | tf_op jit(solution)/shard_map/ppermute | solution.py:96
  86.3 0.1 fusion.26
  86.3 2.6 %collective-permute-start.7 = (bf16[2,256,256]{2,1,0:T(8,128)(2,1)S(1)}, bf16[2,256,256]{2,1,0:T(8,128)(2,1)S(1)}, u32[]{:S(2)}, u32[]{:S(2)}) collective-permute-start(bf16[2,256,256]{2,1,0:T(8,128)(2,1)S(1)} %fusion.26), channel_id=1, source_target_pairs={{0,1},{1,2},{2,3},{3,0},{4,5},{5,6},{6,7},{7,4},{8,9},{9,10},{10,1... | collective-permute-start | bytes 786440 | tf_op jit(solution)/shard_map/ppermute | solution.py:96
  88.9 0.3 collective-permute-done.8
  89.2 0.1 fusion.27
  89.2 0.1 collective-permute-start.9
  89.3 2.7 %collective-permute-done.12 = bf16[2,2,256,256]{3,2,1,0:T(8,128)(2,1)S(1)} collective-permute-done((bf16[2,2,256,256]{3,2,1,0:T(8,128)(2,1)S(1)}, bf16[2,2,256,256]{3,2,1,0:T(8,128)(2,1)S(1)}, u32[]{:S(2)}, u32[]{:S(2)}) %collective-permute-start.12) | collective-permute-done | bytes 524320 | tf_op jit(solution)/shard_map/ppermute | solution.py:96
  92.0 1.6 %collective-permute-start.13 = (bf16[2,256,256]{2,1,0:T(8,128)(2,1)S(1)}, bf16[2,256,256]{2,1,0:T(8,128)(2,1)S(1)}, u32[]{:S(2)}, u32[]{:S(2)}) collective-permute-start(bf16[2,256,256]{2,1,0:T(8,128)(2,1)S(1)} %fusion.28), channel_id=1, source_target_pairs={{0,4},{1,5},{2,6},{3,7},{4,8},{5,9},{6,10},{7,11},{8,12},{9,13},{1... | collective-permute-start | bytes 786440 | tf_op jit(solution)/shard_map/ppermute | solution.py:96
  93.7 1.8 %collective-permute-start.15 = (bf16[2,256,256]{2,1,0:T(8,128)(2,1)S(1)}, bf16[2,256,256]{2,1,0:T(8,128)(2,1)S(1)}, u32[]{:S(2)}, u32[]{:S(2)}) collective-permute-start(bf16[2,256,256]{2,1,0:T(8,128)(2,1)S(1)} %fusion.29), channel_id=1, source_target_pairs={{0,12},{1,13},{2,14},{3,15},{4,0},{5,1},{6,2},{7,3},{8,4},{9,5},{1... | collective-permute-start | bytes 786440 | tf_op jit(solution)/shard_map/ppermute | solution.py:96
  95.5 0.1 fusion.25
  95.6 0.2 collective-permute-done.9
  95.8 0.1 fusion.22
  95.9 3.8 %collective-permute-done.13 = bf16[2,256,256]{2,1,0:T(8,128)(2,1)S(1)} collective-permute-done((bf16[2,256,256]{2,1,0:T(8,128)(2,1)S(1)}, bf16[2,256,256]{2,1,0:T(8,128)(2,1)S(1)}, u32[]{:S(2)}, u32[]{:S(2)}) %collective-permute-start.13) | collective-permute-done | bytes 262176 | tf_op jit(solution)/shard_map/ppermute | solution.py:96
  99.7 0.1 fusion.19
  99.8 0.3 collective-permute-done.15
  100.1 0.1 fusion.16
  100.2 0.3 fusion.4
  100.5 10.8 %psum.14 = f32[514]{0:T(1024)S(1)} all-reduce(f32[514]{0:T(1024)S(1)} %pad_maximum_fusion.6), channel_id=1, replica_groups=mesh['section'=2,'row'=4,'col'=16] {'row'}, use_global_device_ids=true, to_apply=%region_3.4 | all-reduce | flops 514 | bytes 4112 | tf_op jit(solution)/shard_map/psum | solution.py:165
  111.3 0.5 fusion.5
  111.8 0.1 reduce_sum.67
  111.9 0.1 fusion.30
  112.0 14.6 %all_to_all.5 = f32[16,40,128]{2,1,0:T(8,128)S(1)} all-to-all(f32[16,40,128]{2,1,0:T(8,128)S(1)} %broadcast_in_dim.2), channel_id=1, replica_groups=mesh['section'=2,'row'=4,'col'=16] {'col'}, dimensions={0} | all-to-all | bytes 655360 | tf_op jit(solution)/shard_map/all_to_all | solution.py:180
  126.7 0.1 divide_reduce_fusion
  126.8 7.7 %psum.15 = f32[2]{0:T(128)S(1)} all-reduce(f32[2]{0:T(128)S(1)} %get-tuple-element.86), channel_id=1, replica_groups=mesh['section'=2,'row'=4,'col'=16] {'row'}, use_global_device_ids=true, to_apply=%region_8.9 | all-reduce | flops 2 | bytes 16 | tf_op jit(solution)/shard_map/psum | solution.py:190
  134.6 0.6 broadcast_multiply_fusion
  135.2 0.1 rsqrt_multiply_fusion
  135.2 3.7 %multiply_convert_fusion = (bf16[2,256,1024]{2,1,0:T(8,128)(2,1)}, f32[2,256,1024]{2,1,0:T(8,128)}) fusion(f32[2,1024]{1,0:T(2,128)S(1)} %rsqrt_multiply_fusion, f32[2,256]{1,0:T(2,128)S(1)} %get-tuple-element.88, f32[2,256,256]{2,1,0:T(8,128)S(1)} %fusion.16, f32[2,256,256]{2,1,0:T(8,128)S(1)} %fusion.19, f32[2,256,256]{2,1,0:T(8,128)S(1)} %fusion.22, ...), kind=kLoop, calls=%fused_computation.21 | loop fusion | flops 4194304 | bytes 7350280 | tf_op jit(solution)/shard_map/convert_element_type | solution.py:198
  (37 shorter events, 0.5 us)
Async XLA Ops:
  0.7 1.6 %copy-start = (bf16[1024,1024]{1,0:T(8,128)(2,1)S(1)}, bf16[1024,1024]{1,0:T(8,128)(2,1)}, u32[]{:S(2)}) copy-start(bf16[1024,1024]{1,0:T(8,128)(2,1)} %x_ref.11) | copy-start | bytes 6291460
  7.2 21.7 %collective-permute-start = (bf16[4,2,256,256]{3,2,1,0:T(8,128)(2,1)S(1)}, bf16[4,2,256,256]{3,2,1,0:T(8,128)(2,1)S(1)}, u32[]{:S(2)}, u32[]{:S(2)}) collective-permute-start(bf16[4,2,256,256]{3,2,1,0:T(8,128)(2,1)S(1)} %get-tuple-element.68), channel_id=1, source_target_pairs={{0,4},{1,5},{2,6},{3,7},{4,8},{5,9},{6,10},{7,11},{8,12},{9,13},{1... | collective-permute-start | bytes 3145736 | tf_op jit(solution)/shard_map/ppermute | solution.py:96
  8.8 20.8 %collective-permute-start.1 = (bf16[4,2,256,256]{3,2,1,0:T(8,128)(2,1)S(1)}, bf16[4,2,256,256]{3,2,1,0:T(8,128)(2,1)S(1)}, u32[]{:S(2)}, u32[]{:S(2)}) collective-permute-start(bf16[4,2,256,256]{3,2,1,0:T(8,128)(2,1)S(1)} %get-tuple-element.70), channel_id=1, source_target_pairs={{0,12},{1,13},{2,14},{3,15},{4,0},{5,1},{6,2},{7,3},{8,4},{9,5},{1... | collective-permute-start | bytes 3145736 | tf_op jit(solution)/shard_map/ppermute | solution.py:96
  15.5 26.0 %collective-permute-start.2 = (bf16[4,2,256,256]{3,2,1,0:T(8,128)(2,1)S(1)}, bf16[4,2,256,256]{3,2,1,0:T(8,128)(2,1)S(1)}, u32[]{:S(2)}, u32[]{:S(2)}) collective-permute-start(bf16[4,2,256,256]{3,2,1,0:T(8,128)(2,1)S(1)} %get-tuple-element.72), channel_id=1, source_target_pairs={{0,1},{1,2},{2,3},{3,0},{4,5},{5,6},{6,7},{7,4},{8,9},{9,10},{10,1... | collective-permute-start | bytes 3145736 | tf_op jit(solution)/shard_map/ppermute | solution.py:96
  17.5 26.5 %collective-permute-start.3 = (bf16[4,2,256,256]{3,2,1,0:T(8,128)(2,1)S(1)}, bf16[4,2,256,256]{3,2,1,0:T(8,128)(2,1)S(1)}, u32[]{:S(2)}, u32[]{:S(2)}) collective-permute-start(bf16[4,2,256,256]{3,2,1,0:T(8,128)(2,1)S(1)} %get-tuple-element.74), channel_id=1, source_target_pairs={{0,3},{1,0},{2,1},{3,2},{4,7},{5,4},{6,5},{7,6},{8,11},{9,8},{10,9... | collective-permute-start | bytes 3145736 | tf_op jit(solution)/shard_map/ppermute | solution.py:96
  29.3 44.3 %collective-permute-start.4 = (bf16[2,4,2,256,256]{4,3,2,1,0:T(8,128)(2,1)S(1)}, bf16[2,4,2,256,256]{4,3,2,1,0:T(8,128)(2,1)S(1)}, u32[]{:S(2)}, u32[]{:S(2)}) collective-permute-start(bf16[2,4,2,256,256]{4,3,2,1,0:T(8,128)(2,1)S(1)} %fusion.7), channel_id=1, source_target_pairs={{0,4},{1,5},{2,6},{3,7},{4,8},{5,9},{6,10},{7,11},{8,12},{9,13},{1... | collective-permute-start | bytes 6291464 | tf_op jit(solution)/shard_map/ppermute | solution.py:96
  29.9 44.1 %collective-permute-start.5 = (bf16[2,4,2,256,256]{4,3,2,1,0:T(8,128)(2,1)S(1)}, bf16[2,4,2,256,256]{4,3,2,1,0:T(8,128)(2,1)S(1)}, u32[]{:S(2)}, u32[]{:S(2)}) collective-permute-start(bf16[2,4,2,256,256]{4,3,2,1,0:T(8,128)(2,1)S(1)} %fusion.9), channel_id=1, source_target_pairs={{0,12},{1,13},{2,14},{3,15},{4,0},{5,1},{6,2},{7,3},{8,4},{9,5},{1... | collective-permute-start | bytes 6291464 | tf_op jit(solution)/shard_map/ppermute | solution.py:96
  41.8 2.8 %copy-start.1 = (f32[2,256,1024]{2,1,0:T(8,128)S(1)}, f32[2,256,1024]{2,1,0:T(8,128)}, u32[]{:S(2)}) copy-start(f32[2,256,1024]{2,1,0:T(8,128)} %param.15) | copy-start | bytes 6291460
  41.8 36.4 %collective-permute-start.10 = (bf16[2,4,2,256,256]{4,3,2,1,0:T(8,128)(2,1)S(1)}, bf16[2,4,2,256,256]{4,3,2,1,0:T(8,128)(2,1)S(1)}, u32[]{:S(2)}, u32[]{:S(2)}) collective-permute-start(bf16[2,4,2,256,256]{4,3,2,1,0:T(8,128)(2,1)S(1)} %fusion.11), channel_id=1, source_target_pairs={{0,1},{1,2},{2,3},{3,0},{4,5},{5,6},{6,7},{7,4},{8,9},{9,10},{10,1... | collective-permute-start | bytes 6291464 | tf_op jit(solution)/shard_map/ppermute | solution.py:96
  44.2 34.5 %collective-permute-start.11 = (bf16[2,4,2,256,256]{4,3,2,1,0:T(8,128)(2,1)S(1)}, bf16[2,4,2,256,256]{4,3,2,1,0:T(8,128)(2,1)S(1)}, u32[]{:S(2)}, u32[]{:S(2)}) collective-permute-start(bf16[2,4,2,256,256]{4,3,2,1,0:T(8,128)(2,1)S(1)} %fusion.13), channel_id=1, source_target_pairs={{0,3},{1,0},{2,1},{3,2},{4,7},{5,4},{6,5},{7,6},{8,11},{9,8},{10,9... | collective-permute-start | bytes 6291464 | tf_op jit(solution)/shard_map/ppermute | solution.py:96
  75.2 11.1 %collective-permute-start.6 = (bf16[2,2,256,256]{3,2,1,0:T(8,128)(2,1)S(1)}, bf16[2,2,256,256]{3,2,1,0:T(8,128)(2,1)S(1)}, u32[]{:S(2)}, u32[]{:S(2)}) collective-permute-start(bf16[2,2,256,256]{3,2,1,0:T(8,128)(2,1)S(1)} %pad_maximum_fusion.1), channel_id=1, source_target_pairs={{0,1},{1,2},{2,3},{3,0},{4,5},{5,6},{6,7},{7,4},{8,9},{9,10},{10,1... | collective-permute-start | bytes 1572872 | tf_op jit(solution)/shard_map/ppermute | solution.py:96
  78.1 11.1 %collective-permute-start.8 = (bf16[2,2,256,256]{3,2,1,0:T(8,128)(2,1)S(1)}, bf16[2,2,256,256]{3,2,1,0:T(8,128)(2,1)S(1)}, u32[]{:S(2)}, u32[]{:S(2)}) collective-permute-start(bf16[2,2,256,256]{3,2,1,0:T(8,128)(2,1)S(1)} %pad_maximum_fusion.2), channel_id=1, source_target_pairs={{0,3},{1,0},{2,1},{3,2},{4,7},{5,4},{6,5},{7,6},{8,11},{9,8},{10,9... | collective-permute-start | bytes 1572872 | tf_op jit(solution)/shard_map/ppermute | solution.py:96
  80.0 12.0 %collective-permute-start.12 = (bf16[2,2,256,256]{3,2,1,0:T(8,128)(2,1)S(1)}, bf16[2,2,256,256]{3,2,1,0:T(8,128)(2,1)S(1)}, u32[]{:S(2)}, u32[]{:S(2)}) collective-permute-start(bf16[2,2,256,256]{3,2,1,0:T(8,128)(2,1)S(1)} %pad_maximum_fusion.3), channel_id=1, source_target_pairs={{0,4},{1,5},{2,6},{3,7},{4,8},{5,9},{6,10},{7,11},{8,12},{9,13},{1... | collective-permute-start | bytes 1572872 | tf_op jit(solution)/shard_map/ppermute | solution.py:96
  81.6 12.0 %collective-permute-start.14 = (bf16[2,2,256,256]{3,2,1,0:T(8,128)(2,1)S(1)}, bf16[2,2,256,256]{3,2,1,0:T(8,128)(2,1)S(1)}, u32[]{:S(2)}, u32[]{:S(2)}) collective-permute-start(bf16[2,2,256,256]{3,2,1,0:T(8,128)(2,1)S(1)} %pad_maximum_fusion.4), channel_id=1, source_target_pairs={{0,12},{1,13},{2,14},{3,15},{4,0},{5,1},{6,2},{7,3},{8,4},{9,5},{1... | collective-permute-start | bytes 1572872 | tf_op jit(solution)/shard_map/ppermute | solution.py:96
  86.3 9.1 %collective-permute-start.7 = (bf16[2,256,256]{2,1,0:T(8,128)(2,1)S(1)}, bf16[2,256,256]{2,1,0:T(8,128)(2,1)S(1)}, u32[]{:S(2)}, u32[]{:S(2)}) collective-permute-start(bf16[2,256,256]{2,1,0:T(8,128)(2,1)S(1)} %fusion.26), channel_id=1, source_target_pairs={{0,1},{1,2},{2,3},{3,0},{4,5},{5,6},{6,7},{7,4},{8,9},{9,10},{10,1... | collective-permute-start | bytes 786440 | tf_op jit(solution)/shard_map/ppermute | solution.py:96
  89.2 6.5 %collective-permute-start.9 = (bf16[2,256,256]{2,1,0:T(8,128)(2,1)S(1)}, bf16[2,256,256]{2,1,0:T(8,128)(2,1)S(1)}, u32[]{:S(2)}, u32[]{:S(2)}) collective-permute-start(bf16[2,256,256]{2,1,0:T(8,128)(2,1)S(1)} %fusion.27), channel_id=1, source_target_pairs={{0,3},{1,0},{2,1},{3,2},{4,7},{5,4},{6,5},{7,6},{8,11},{9,8},{10,9... | collective-permute-start | bytes 786440 | tf_op jit(solution)/shard_map/ppermute | solution.py:96
  92.0 7.7 %collective-permute-start.13 = (bf16[2,256,256]{2,1,0:T(8,128)(2,1)S(1)}, bf16[2,256,256]{2,1,0:T(8,128)(2,1)S(1)}, u32[]{:S(2)}, u32[]{:S(2)}) collective-permute-start(bf16[2,256,256]{2,1,0:T(8,128)(2,1)S(1)} %fusion.28), channel_id=1, source_target_pairs={{0,4},{1,5},{2,6},{3,7},{4,8},{5,9},{6,10},{7,11},{8,12},{9,13},{1... | collective-permute-start | bytes 786440 | tf_op jit(solution)/shard_map/ppermute | solution.py:96
  93.7 6.4 %collective-permute-start.15 = (bf16[2,256,256]{2,1,0:T(8,128)(2,1)S(1)}, bf16[2,256,256]{2,1,0:T(8,128)(2,1)S(1)}, u32[]{:S(2)}, u32[]{:S(2)}) collective-permute-start(bf16[2,256,256]{2,1,0:T(8,128)(2,1)S(1)} %fusion.29), channel_id=1, source_target_pairs={{0,12},{1,13},{2,14},{3,15},{4,0},{5,1},{6,2},{7,3},{8,4},{9,5},{1... | collective-permute-start | bytes 786440 | tf_op jit(solution)/shard_map/ppermute | solution.py:96
  99.8 11.5 %copy-start.5 = (f32[2,256]{1,0:T(2,128)S(1)}, f32[2,256]{1,0:T(2,128)}, u32[]{:S(2)}) copy-start(f32[2,256]{1,0:T(2,128)} %param.16) | copy-start | bytes 6148
  100.5 26.2 %copy-start.4 = (f32[2,1024]{1,0:T(2,128)S(1)}, f32[2,1024]{1,0:T(2,128)}, u32[]{:S(2)}) copy-start(f32[2,1024]{1,0:T(2,128)} %param.17) | copy-start | bytes 24580
  111.3 27.6 %copy-start.3 = (f32[2,256]{1,0:T(2,128)}, f32[2,256]{1,0:T(2,128)S(1)}, u32[]{:S(2)}) copy-start(f32[2,256]{1,0:T(2,128)S(1)} %get-tuple-element.89) | copy-start | bytes 6148
  126.8 12.1 %copy-start.2 = (f32[2,1024]{1,0:T(2,128)}, f32[2,1024]{1,0:T(2,128)S(1)}, u32[]{:S(2)}) copy-start(f32[2,1024]{1,0:T(2,128)S(1)} %get-tuple-element.87) | copy-start | bytes 24580
